TPU v7x, 128 devices: a whole 4x4x4 slice. The times are simulated.
128 devices in a mesh: row: 8 (over z_lo, y), col: 16 (over x, z_hi, core).
Axes of the slice: x: 4, y: 4, z: 4 (z_hi: 2, z_lo: 2; z = z_hi * 2 + z_lo), core: 2. Of those that a mesh axis runs over, the one named last changes fastest.
Arguments:
- positions: int32 [8, 16, 16, 2], P('row', 'col'), may hold values from -128 to 3967, as said below
- counts: int32 [8, 16], P('row', 'col'), may hold values from 1 to 16, as said below
- amplitudes: bfloat16 [8, 16, 16, 256, 256], P('row', 'col'), may hold values from 0.19921875 to 5
- object_field: float32 [2, 2048, 4096], P(None, 'row', 'col'), may hold values from -6 to 6
- probe: float32 [2, 256, 256], replicated, may hold values from -6 to 6
Outputs:
- object_new: float32 [2, 2048, 4096], P(None, 'row', 'col')
- probe_new: float32 [2, 256, 256], replicated
Inputs may be any that keep to these rules, and one draw needn't show every extreme that they name: `positions`: slot k of tile (i, j) holds the corner of a patch whose centre (corner plus 256/2 in each coordinate) lies in that tile: rows i * 256 to (i + 1) * 256 - 1 and columns j * 256 to (j + 1) * 256 - 1. Slots at or beyond the tile's count are not read. `counts`: some tile has exactly 16 live positions.
All inputs are finite; a program needn't handle non-finite values.
Results may differ from a plain program's by a relative error of at most 0.0039.
Values sent between devices are 32-bit elements; how exact they have to be, the bound alone decides.
A program may use at most 192 MiB of HBM per device.

v0:
```python
import math

import jax
import jax.numpy as jnp
from jax import lax
from jax.sharding import PartitionSpec as P

F = 256
ITERS = 2


def with_halo(cells, sides, width):
    for axis, dim in sides:
        count = lax.axis_size(axis)
        ends = count - 1
        head = lax.slice_in_dim(cells, 0, width, axis=dim)
        tail = lax.slice_in_dim(cells, cells.shape[dim] - width, cells.shape[dim], axis=dim)
        cells = jnp.concatenate(
            [
                lax.ppermute(tail, axis, [(i, (i + 1) % count) for i in range(ends)]),
                cells,
                lax.ppermute(head, axis, [((i + 1) % count, i) for i in range(ends)]),
            ],
            axis=dim,
        )
    return cells


def shifted(block, axis, distance):
    devices = range(lax.axis_size(axis))
    route = [(i - distance, i) for i in devices if i - distance in devices]
    return lax.ppermute(block, axis, route)


def dft_tables():
    counter = jnp.arange(F, dtype=jnp.int32)
    phases = counter[:, None] * counter[None, :] % F
    angles = phases.astype(jnp.float32) * (2.0 * math.pi / F)
    factor = 1.0 / math.sqrt(F)
    table_re = (jnp.cos(angles) * factor).astype(jnp.bfloat16)
    table_im = (-jnp.sin(angles) * factor).astype(jnp.bfloat16)
    return (table_re, table_im)


def complex_product(left_re, left_im, right_re, right_im):
    order_size = left_re.shape[0]
    stacked = jnp.dot(
        jnp.concatenate([left_re, left_im], 0),
        jnp.concatenate([right_re, right_im], 1),
        preferred_element_type=jnp.float32,
    )
    real_part = stacked[:order_size, :order_size] - stacked[order_size:, order_size:]
    imag_part = stacked[:order_size, order_size:] + stacked[order_size:, :order_size]
    return (real_part, imag_part)


def slot_update(patch_cells, amplitude, probe, table_re, table_im):
    probe_re = probe[0]
    probe_im = probe[1]
    patch_re = patch_cells[0]
    patch_im = patch_cells[1]
    exit_re = (probe_re * patch_re - probe_im * patch_im).astype(jnp.bfloat16)
    exit_im = (probe_re * patch_im + probe_im * patch_re).astype(jnp.bfloat16)
    half_re, half_im = complex_product(table_re, table_im, exit_re, exit_im)
    far_re, far_im = complex_product(
        half_re.astype(jnp.bfloat16), half_im.astype(jnp.bfloat16), table_re, table_im
    )
    ratio_term = amplitude.astype(jnp.float32) / jnp.sqrt(far_re * far_re + far_im * far_im + 1.0)
    miss_re = (far_re - ratio_term * far_re).astype(jnp.bfloat16)
    miss_im = (far_im - ratio_term * far_im).astype(jnp.bfloat16)
    back_re, back_im = complex_product(table_re, -table_im, miss_re, miss_im)
    chi_re, chi_im = complex_product(
        back_re.astype(jnp.bfloat16), back_im.astype(jnp.bfloat16), table_re, -table_im
    )
    object_grad = jnp.stack(
        [probe_re * chi_re + probe_im * chi_im, probe_re * chi_im - probe_im * chi_re]
    )
    probe_grad = jnp.stack(
        [patch_re * chi_re + patch_im * chi_im, patch_re * chi_im - patch_im * chi_re]
    )
    weight = patch_re * patch_re + patch_im * patch_im
    return (object_grad, probe_grad, weight)


def add_patch(gradient, update, corner_row, corner_col):
    zero_index = jnp.zeros((), jnp.int32)
    present = lax.dynamic_slice(gradient, (zero_index, corner_row, corner_col), update.shape)
    return lax.dynamic_update_slice(
        gradient, present + update, (zero_index, corner_row, corner_col)
    )


def body(positions, counts, amplitudes, object_field, probe):
    half_width = F // 2
    tile_rows = object_field.shape[1]
    tile_cols = object_field.shape[2]
    table_re, table_im = dft_tables()
    anchor = jnp.stack(
        [
            lax.axis_index("row") * tile_rows - half_width,
            lax.axis_index("col") * tile_cols - half_width,
        ]
    )
    corners = positions[0, 0] - anchor[None, :]
    own_load = counts[0, 0]
    measured = amplitudes[0, 0]
    zero_index = jnp.zeros((), jnp.int32)
    for iteration in range(ITERS):
        extended = with_halo(object_field, (("row", 1), ("col", 2)), half_width)
        coverage = probe[0] * probe[0] + probe[1] * probe[1]
        current_probe = probe

        def own_slot(slot_index, carried):
            gradient, probe_sum, weight_sum = carried
            patch_cells = lax.dynamic_slice(
                extended, (zero_index, corners[slot_index, 0], corners[slot_index, 1]), (2, F, F)
            )
            object_grad, probe_grad, weight = slot_update(
                patch_cells, measured[slot_index], current_probe, table_re, table_im
            )
            update = jnp.concatenate([object_grad, coverage[None]], 0)
            gradient = add_patch(gradient, update, corners[slot_index, 0], corners[slot_index, 1])
            return (gradient, probe_sum + probe_grad, weight_sum + weight)

        initial = (
            jnp.zeros((3, tile_rows + F, tile_cols + F), jnp.float32),
            jnp.zeros((2, F, F), jnp.float32),
            jnp.zeros((F, F), jnp.float32),
        )
        gradient, probe_sum, weight_sum = lax.fori_loop(0, own_load, own_slot, initial)
        inner_rows = gradient[:, half_width : half_width + tile_rows, :]
        for offset in (1, -1):
            rim_strip = (
                gradient[:, half_width + tile_rows :, :]
                if offset == 1
                else gradient[:, :half_width, :]
            )
            arrived = shifted(rim_strip, "row", offset)
            inner_rows = (
                inner_rows.at[:, :half_width, :].add(arrived)
                if offset == 1
                else inner_rows.at[:, tile_rows - half_width :, :].add(arrived)
            )
        own_cells = inner_rows[:, :, half_width : half_width + tile_cols]
        for offset in (1, -1):
            rim_strip = (
                inner_rows[:, :, half_width + tile_cols :]
                if offset == 1
                else inner_rows[:, :, :half_width]
            )
            arrived = shifted(rim_strip, "col", offset)
            own_cells = (
                own_cells.at[:, :, :half_width].add(arrived)
                if offset == 1
                else own_cells.at[:, :, tile_cols - half_width :].add(arrived)
            )
        object_field = object_field - own_cells[:2] / (own_cells[2] + 1.0)
        grad_total, weight_total = lax.psum((probe_sum, weight_sum), ("row", "col"))
        probe = probe - grad_total / (weight_total + 1.0)
    return (object_field, probe)


def solution(mesh):
    return jax.shard_map(
        body,
        mesh=mesh,
        in_specs=(
            P("row", "col", None, None),
            P("row", "col"),
            P("row", "col", None, None, None),
            P(None, "row", "col"),
            P(),
        ),
        out_specs=(P(None, "row", "col"), P()),
        check_vma=False,
    )
```

profile of v0, /device:TPU:1, one launch (start us, length us, event | category | flops | bytes accessed | tf_op | source)
XLA Modules:
  0.0 1265.0 jit_solution(7799937843583621039)
XLA Ops:
  7.2 1.9 fusion.90
  10.4 4.7 collective-permute-start
  18.9 2.4 copy.7
  21.5 6.8 collective-permute-start.2
  28.3 1.9 collective-permute-start.3
  31.1 8.9 collective-permute-done.2
  42.1 2.0 broadcast.152.clone
  44.1 420.5 %while.40 = (s32[]{:T(128)}, f32[3,512,512]{2,1,0:T(8,128)}, f32[2,256,256]{2,1,0:T(8,128)}, f32[256,256]{1,0:T(8,128)}, s32[]{:T(128)}, /*index=5*/s32[16,2]{0,...) while((s32[]{:T(128)}, f32[3,512,512]{2,1,0:T(8,128)}, ...), condition=%wide.region_1.2_spmd, body=%wide.region_0.1_spmd.sunk | while | flops 542965760 | bytes 22413680 | solution.py:130
  61.3 9.1 dynamic_update_slice.12
  87.6 8.7 dynamic_update_slice.12
  113.5 8.5 dynamic_update_slice.12
  139.2 9.4 dynamic_update_slice.12
  165.8 9.1 dynamic_update_slice.12
  192.1 9.1 dynamic_update_slice.12
  218.5 9.5 dynamic_update_slice.12
  245.2 8.5 dynamic_update_slice.12
  271.0 9.2 dynamic_update_slice.12
  297.4 9.2 dynamic_update_slice.12
  323.8 9.1 dynamic_update_slice.12
  350.1 8.9 dynamic_update_slice.12
  376.2 9.1 dynamic_update_slice.12
  402.5 9.4 dynamic_update_slice.12
  429.1 8.5 dynamic_update_slice.12
  454.8 9.2 dynamic_update_slice.12
  469.1 7.4 collective-permute-done.4
  476.6 5.5 collective-permute-done.5
  482.4 1.9 collective-permute-start.6
  484.4 2.6 collective-permute-start.7
  487.0 2.0 collective-permute-done.6
  489.1 6.4 collective-permute-done.7
  495.8 15.2 %collective-permute-start.8 = (f32[2,128,256]{2,1,0:T(8,128)S(1)}, f32[2,128,256]{2,1,0:T(8,128)S(1)}, u32[]{:S(2)}, u32[]{:S(2)}) collective-permute-start(f32[2,128,256]{2,1,0:T(8,128)S(1)} %get-tuple-element.522), channel_id=1, source_target_pairs={{0,16},{16,32},{32,48},{48,64},{64,80},{80,96},{96,112},{1,17},{17... | collective-permute-start | bytes 786440 | tf_op jit(solution)/shard_map/ppermute | solution.py:20
  512.4 1.9 collective-permute-done.8
  514.3 3.8 collective-permute-done.9
  518.8 4.3 collective-permute-start.10
  523.2 1.9 collective-permute-start.11
  525.1 136.0 %all-reduce.7.cloned.1.call-done = (f32[2,256,256]{2,1,0:T(8,128)}, f32[256,256]{1,0:T(8,128)}) async-done(((f32[2,256,256]{2,1,0:T(8,128)}, f32[256,256]{1,0:T(8,128)}), (f32[2,256,256]{2,1,0:T(8,128)}, f32[256,256]{1,0:T(8,128)})) %all-reduce.7.cloned.1.call-update) | async-done | bytes 786448 | tf_op jit(solution)/shard_map/psum | solution.py:158
  667.0 2.0 broadcast.152
  669.1 421.5 %while.41 = (s32[]{:T(128)}, f32[3,512,512]{2,1,0:T(8,128)}, f32[2,256,256]{2,1,0:T(8,128)}, f32[256,256]{1,0:T(8,128)}, s32[]{:T(128)}, /*index=5*/s32[16,2]{0,...) while((s32[]{:T(128)}, f32[3,512,512]{2,1,0:T(8,128)}, ...), condition=%wide.region_5.6_spmd, body=%wide.region_4.5_spmd.sunk | while | flops 542965760 | bytes 22413680 | solution.py:130
  686.3 9.1 dynamic_update_slice.13
  710.8 1.9 maximum_add_fusion.11
  712.7 8.7 dynamic_update_slice.13
  738.6 8.5 dynamic_update_slice.13
  764.4 9.4 dynamic_update_slice.13
  791.1 9.1 dynamic_update_slice.13
  817.5 9.1 dynamic_update_slice.13
  843.9 9.5 dynamic_update_slice.13
  870.7 8.5 dynamic_update_slice.13
  896.5 9.2 dynamic_update_slice.13
  922.9 9.2 dynamic_update_slice.13
  949.4 9.1 dynamic_update_slice.13
  975.8 8.9 dynamic_update_slice.13
  1002.0 9.1 dynamic_update_slice.13
  1028.3 9.4 dynamic_update_slice.13
  1054.9 8.5 dynamic_update_slice.13
  1080.7 9.2 dynamic_update_slice.13
  1090.5 2.6 fusion.83
  1093.1 2.2 collective-permute-start.12
  1096.7 6.9 collective-permute-done.12
  1105.2 3.0 collective-permute-done.13
  1109.5 1.9 collective-permute-start.14
  1111.4 134.1 %all-reduce.5.cloned.1.call-done = (f32[2,256,256]{2,1,0:T(8,128)}, f32[256,256]{1,0:T(8,128)}) async-done(((f32[2,256,256]{2,1,0:T(8,128)}, f32[256,256]{1,0:T(8,128)}), (f32[2,256,256]{2,1,0:T(8,128)}, f32[256,256]{1,0:T(8,128)})) %all-reduce.5.cloned.1.call-update) | async-done | bytes 786448 | tf_op jit(solution)/shard_map/psum | solution.py:158
  1246.5 2.9 collective-permute-start.15
  1249.5 1.9 divide_subtract_fusion
  1251.6 5.6 collective-permute-done.15
  (501 shorter events, 435.3 us)
Async XLA Ops:
  7.2 11.8 copy-start.8
  7.2 654.0 %all-reduce.7.cloned.1.call-start = ((), (), s32[]{:S(2)}) async-start(), calls=%async_computation.1 | async-start | bytes 1572864 | tf_op jit(solution)/shard_map/psum | solution.py:158
  9.1 12.2 collective-permute-start.1
  10.4 10.9 collective-permute-start
  18.9 2.4 copy-start.6
  21.3 9.0 copy-start.13
  21.3 9.1 copy-start
  21.5 18.5 %collective-permute-start.2 = (f32[2,512,128]{2,1,0:T(8,128)S(1)}, f32[2,512,128]{2,1,0:T(8,128)S(1)}, u32[]{:S(2)}, u32[]{:S(2)}) collective-permute-start(f32[2,512,128]{2,1,0:T(8,128)S(1)} %get-tuple-element.520), channel_id=1, source_target_pairs={{0,1},{1,2},{2,3},{3,4},{4,5},{5,6},{6,7},{7,8},{8,9},{9,10},{10,1... | collective-permute-start | bytes 1572872 | tf_op jit(solution)/shard_map/ppermute | solution.py:20
  28.3 12.0 collective-permute-start.3
  464.6 4.3 copy-start.2
  466.3 10.2 collective-permute-start.4
  467.6 14.5 %collective-permute-start.5 = (f32[3,128,512]{2,1,0:T(8,128)S(1)}, f32[3,128,512]{2,1,0:T(8,128)S(1)}, u32[]{:S(2)}, u32[]{:S(2)}) collective-permute-start(f32[3,128,512]{2,1,0:T(8,128)S(1)} %get-tuple-element.512), channel_id=1, source_target_pairs={{16,0},{32,16},{48,32},{64,48},{80,64},{96,80},{112,96},{17,1},{33... | collective-permute-start | bytes 2359304 | tf_op jit(solution)/shard_map/ppermute | solution.py:32
  482.4 6.6 collective-permute-start.6
  484.3 11.3 copy-start.7
  484.4 11.2 collective-permute-start.7
  495.8 22.6 %copy-start.3 = (f32[2,256,256]{2,1,0:T(8,128)}, f32[2,256,256]{2,1,0:T(8,128)S(1)}, u32[]{:S(2)}) copy-start(f32[2,256,256]{2,1,0:T(8,128)S(1)} %fusion.67) | copy-start | bytes 1572868
  495.8 18.5 %collective-permute-start.8 = (f32[2,128,256]{2,1,0:T(8,128)S(1)}, f32[2,128,256]{2,1,0:T(8,128)S(1)}, u32[]{:S(2)}, u32[]{:S(2)}) collective-permute-start(f32[2,128,256]{2,1,0:T(8,128)S(1)} %get-tuple-element.522), channel_id=1, source_target_pairs={{0,16},{16,32},{32,48},{48,64},{64,80},{80,96},{96,112},{1,17},{17... | collective-permute-start | bytes 786440 | tf_op jit(solution)/shard_map/ppermute | solution.py:20
  511.0 7.1 collective-permute-start.9
  512.4 733.2 %all-reduce.5.cloned.1.call-start = ((), (), s32[]{:S(2)}) async-start(), calls=%async_computation | async-start | bytes 1572864 | tf_op jit(solution)/shard_map/psum | solution.py:158
  514.3 4.0 copy-start.9
  518.2 0.7 copy-start.11
  518.8 145.2 %collective-permute-start.10 = (f32[2,512,128]{2,1,0:T(8,128)S(1)}, f32[2,512,128]{2,1,0:T(8,128)}, u32[]{:S(2)}, u32[]{:S(2)}) collective-permute-start(f32[2,512,128]{2,1,0:T(8,128)S(1)} %get-tuple-element.518), channel_id=1, source_target_pairs={{0,1},{1,2},{2,3},{3,4},{4,5},{5,6},{6,7},{7,8},{8,9},{9,10},{10,1... | collective-permute-start | bytes 1572872 | tf_op jit(solution)/shard_map/ppermute | solution.py:20
  523.2 140.9 %collective-permute-start.11 = (f32[2,512,128]{2,1,0:T(8,128)S(1)}, f32[2,512,128]{2,1,0:T(8,128)}, u32[]{:S(2)}, u32[]{:S(2)}) collective-permute-start(f32[2,512,128]{2,1,0:T(8,128)S(1)} %get-tuple-element.519), channel_id=1, source_target_pairs={{1,0},{2,1},{3,2},{4,3},{5,4},{6,5},{7,6},{8,7},{9,8},{10,9},{11,1... | collective-permute-start | bytes 1572872 | tf_op jit(solution)/shard_map/ppermute | solution.py:22
  661.1 2.9 copy-start.4
  661.1 2.9 copy-start.10
  661.1 3.0 copy-start.12
  1090.5 6.0 copy-start.1
  1093.1 10.5 collective-permute-start.12
  1095.3 12.8 %collective-permute-start.13 = (f32[3,128,512]{2,1,0:T(8,128)S(1)}, f32[3,128,512]{2,1,0:T(8,128)}, u32[]{:S(2)}, u32[]{:S(2)}) collective-permute-start(f32[3,128,512]{2,1,0:T(8,128)S(1)} %get-tuple-element.510), channel_id=1, source_target_pairs={{16,0},{32,16},{48,32},{64,48},{80,64},{96,80},{112,96},{17,1},{33... | collective-permute-start | bytes 2359304 | tf_op jit(solution)/shard_map/ppermute | solution.py:32
  1109.5 142.0 %collective-permute-start.14 = (f32[3,256,128]{2,1,0:T(8,128)S(1)}, f32[3,256,128]{2,1,0:T(8,128)S(1)}, u32[]{:S(2)}, u32[]{:S(2)}) collective-permute-start(f32[3,256,128]{2,1,0:T(8,128)S(1)} %get-tuple-element.515), channel_id=1, source_target_pairs={{0,1},{1,2},{2,3},{3,4},{4,5},{5,6},{6,7},{7,8},{8,9},{9,10},{10,1... | collective-permute-start | bytes 1179656 | tf_op jit(solution)/shard_map/ppermute | solution.py:32
  1246.5 10.6 collective-permute-start.15
  1251.4 5.9 copy-start.5
Sparse Core Ops, SparseCore 0:
  512.5 148.5 all-reduce.6
  1096.9 148.6 all-reduce.4
where the time goes:
time: 1290 us; the launch traced here: 1260 us
  local copies, waits for them, and re-layouts  327 us (25%)
  waiting for transfers between devices  322 us (25%)
  other arithmetic  244 us (19%)
  matrix products  162 us (13%)
  loops' own time  144 us (11%)
  starting transfers between devices  52.9 us (4%)
  between operations  14.5 us (1%)
    dynamic_update_slice x32, local copies, waits for them, and re-layouts, add_patch(): lax.dynamic_update_slice(gradient, present + update, (zero_index, corner_...  289 us
    psum x2, waiting for transfers between devices, body(): grad_total, weight_total = lax.psum((probe_sum, weight_sum), ('row', 'col'))  270 us
    dot_general x128, matrix products, complex_product(): jnp.dot(jnp.concatenate([left_re, left_im], 0), jnp.concatenate([right_re...  162 us
    another operation x2, loops' own time, body(): lax.fori_loop(0, own_load, own_slot, initial)  144 us
    add x32, other arithmetic, own_slot(): return (gradient, probe_sum + probe_grad, weight_sum + weight)  61 us
    another operation x32, other arithmetic, slot_update(): jnp.stack([patch_re * chi_re + patch_im * chi_im, patch_re * chi_im - pat...  60.4 us
    add x32, other arithmetic, add_patch(): present + update  53.6 us
    ppermute x8, waiting for transfers between devices, shifted(): return lax.ppermute(block, axis, route)  36.8 us
  transfers between devices with their start and end apart: 18, of which 13 were waited for; matrix products, arithmetic and copies ran while one was open for 1% of the time, Pallas kernels for 0%

commit v1 on v0

v1 whole, which is shorter than its diff:
```python
import functools, math
import numpy as np
import jax, jax.numpy as jnp
from jax import lax
from jax.experimental import pallas as pl
from jax.experimental.pallas import tpu as pltpu
from jax.sharding import PartitionSpec as P

F = 256
ITERS = 2
f32=jnp.float32; bf16=jnp.bfloat16

def tables():
    c=np.arange(F,dtype=np.int32)
    ang=(c[:,None]*c[None,:]%F).astype(np.float32)*np.float32(2*math.pi/F)
    re=(np.cos(ang)/np.float32(16)).astype(np.float32)
    im=(-np.sin(ang)/np.float32(16)).astype(np.float32)
    fwd=np.block([[re,-im],[im,re]]); inv=np.block([[re,im],[-im,re]])
    return jnp.asarray(fwd,bf16), jnp.asarray(inv,bf16)

CH=16
def slots_kernel(corner, load, amp, ext, probe, fwd, inv, grad, psum,
                 patch, cov, exit_s, half_s, miss_s, chi_s):
    grad[...]=jnp.zeros(grad.shape,f32)
    psum[...]=jnp.zeros(psum.shape,f32)
    cov[...]=probe[0]*probe[0]+probe[1]*probe[1]
    lane=lax.broadcasted_iota(jnp.int32,(CH,128),1)
    def slot(k,_):
        r=corner[k,0]; c=corner[k,1]
        q=c//128; s=c-q*128
        back=jnp.where(s==0,0,128-s)
        keep=lane<128-s
        for i in range(F//CH):
            rows=pl.ds(i*CH,CH)
            got=[]
            for ch in range(2):
                t=[pltpu.roll(ext[ch,q+j,pl.ds(r+i*CH,CH),:],back,1) for j in range(3)]
                got.append(jnp.concatenate([jnp.where(keep,t[0],t[1]),jnp.where(keep,t[1],t[2])],1))
            re,im=got
            patch[0,rows,:]=re; patch[1,rows,:]=im
            pr=probe[0,rows,:]; pi=probe[1,rows,:]
            exit_s[rows,:]=(pr*re-pi*im).astype(bf16)
            exit_s[pl.ds(F+i*CH,CH),:]=(pr*im+pi*re).astype(bf16)
            psum[2,rows,:]+=re*re+im*im
        half=jnp.dot(fwd[...],exit_s[...],preferred_element_type=f32).astype(bf16)
        half_s[:,:F]=half[:F]; half_s[:,F:]=half[F:]
        far=jnp.dot(half_s[...],inv[...],preferred_element_type=f32)
        fr=far[:,:F]; fi=far[:,F:]
        ratio=1.0-amp[k].astype(f32)*lax.rsqrt(fr*fr+fi*fi+1.0)
        miss_s[:F,:]=(fr*ratio).astype(bf16)
        miss_s[F:,:]=(fi*ratio).astype(bf16)
        back_=jnp.dot(inv[...],miss_s[...],preferred_element_type=f32).astype(bf16)
        half_s[:,:F]=back_[:F]; half_s[:,F:]=back_[F:]
        chi_s[...]=jnp.dot(half_s[...],fwd[...],preferred_element_type=f32)
        put=lane>=s
        for i in range(F//CH):
            rows=pl.ds(i*CH,CH)
            cr=chi_s[rows,:F]; ci=chi_s[rows,F:]
            pr=probe[0,rows,:]; pi=probe[1,rows,:]
            re=patch[0,rows,:]; im=patch[1,rows,:]
            psum[0,rows,:]+=re*cr+im*ci
            psum[1,rows,:]+=re*ci-im*cr
            for ch,u in ((0,pr*cr+pi*ci),(1,pr*ci-pi*cr),(2,cov[rows,:])):
                u0=pltpu.roll(u[:,:128],s,1); u1=pltpu.roll(u[:,128:],s,1)
                at=pl.ds(r+i*CH,CH)
                grad[ch,q,at,:]+=jnp.where(put,u0,0.0)
                grad[ch,q+1,at,:]+=jnp.where(put,u1,u0)
                grad[ch,q+2,at,:]+=jnp.where(put,0.0,u1)
        return 0
    lax.fori_loop(0,load[0],slot,0)

def slots(corner,load,amp,ext,probe,fwd,inv):
    V=pl.BlockSpec(memory_space=pltpu.VMEM); S=pl.BlockSpec(memory_space=pltpu.SMEM)
    return pl.pallas_call(slots_kernel,
        out_shape=(jax.ShapeDtypeStruct((3,4,512,128),f32),jax.ShapeDtypeStruct((3,F,F),f32)),
        in_specs=[S,S,V,V,V,V,V], out_specs=(V,V),
        scratch_shapes=[pltpu.VMEM((2,F,F),f32),pltpu.VMEM((F,F),f32),pltpu.VMEM((2*F,F),bf16),
            pltpu.VMEM((F,2*F),bf16),pltpu.VMEM((2*F,F),bf16),pltpu.VMEM((F,2*F),f32)],
        compiler_params=pltpu.CompilerParams(vmem_limit_bytes=48*2**20),
    )(corner,load,amp,ext,probe,fwd,inv)
MESH = pl.DeviceIdType.MESH
HALF = F // 2
TILE = slice(HALF, HALF + F)


class Places:
    def __init__(self):
        row, col = lax.axis_index("row"), lax.axis_index("col")
        n_row, n_col = lax.axis_size("row"), lax.axis_size("col")
        self.row, self.col, self.n_row, self.n_col = row, col, n_row, n_col
        z_lo, self.y = row // 4, row % 4
        self.x, z_hi, self.core = col // 4, col // 2 % 2, col % 2
        self.z = z_hi * 2 + z_lo
        self.up, self.down = ((row + n_row - 1) % n_row, col), ((row + 1) % n_row, col)
        self.left, self.right = (row, (col + n_col - 1) % n_col), (row, (col + 1) % n_col)
        self.sides = (self.up, self.down, self.left, self.right)
        self.twin = (row, col + 1 - 2 * self.core)
        self.along_x = [(row, (self.x + d) % 4 * 4 + col % 4) for d in (1, 2, 3)]
        self.along_y = [(z_lo * 4 + (self.y + d) % 4, col) for d in (1, 2, 3)]
        self.along_z = []
        for d in (1, 2, 3):
            z = (self.z + d) % 4
            self.along_z.append((z % 2 * 4 + self.y, self.x * 4 + z // 2 * 2 + self.core))


def meet(peers):
    barrier = pltpu.get_barrier_semaphore()
    for peer in peers:
        pl.semaphore_signal(barrier, inc=1, device_id=peer, device_id_type=MESH)
    pl.semaphore_wait(barrier, len(peers))


class Sender:
    def __init__(self, send_sem, recv_sem):
        self.send_sem, self.recv_sem, self.used = send_sem, recv_sem, 0
        self.open = []

    def __call__(self, src, dst, peer):
        copy = pltpu.make_async_remote_copy(
            src_ref=src,
            dst_ref=dst,
            send_sem=self.send_sem.at[self.used],
            recv_sem=self.recv_sem.at[self.used],
            device_id=peer,
            device_id_type=MESH,
        )
        self.used += 1
        copy.start()
        self.open.append(copy)
        return copy

    def close(self):
        for copy in self.open:
            copy.wait_send()


def arrive(copies):
    for copy in copies:
        copy.wait_recv()


TOP, BOTTOM = pl.ds(HALF, HALF), pl.ds(F, HALF)
ABOVE, BELOW = pl.ds(0, HALF), pl.ds(F + HALF, HALF)
INNER, BOTH, ALL = pl.ds(HALF, F), pl.ds(1, 2), pl.ds(0, 4)


def halo_first(send, at, ext):
    return [
        send(ext.at[0, BOTH, TOP, :], ext.at[0, BOTH, BELOW, :], at.up),
        send(ext.at[0, BOTH, BOTTOM, :], ext.at[0, BOTH, ABOVE, :], at.down),
        send(ext.at[1, 1, INNER, :], ext.at[1, 3, INNER, :], at.left),
        send(ext.at[1, 2, INNER, :], ext.at[1, 0, INNER, :], at.right),
    ]


def halo_second(send, at, ext):
    return [
        send(ext.at[0, 1, :, :], ext.at[0, 3, :, :], at.left),
        send(ext.at[0, 2, :, :], ext.at[0, 0, :, :], at.right),
        send(ext.at[1, ALL, TOP, :], ext.at[1, ALL, BELOW, :], at.up),
        send(ext.at[1, ALL, BOTTOM, :], ext.at[1, ALL, ABOVE, :], at.down),
    ]


def clear_outside(at, ext):
    @pl.when(at.row == 0)
    def _():
        ext[:, :, :HALF, :] = jnp.zeros((2, 4, HALF, 128), f32)

    @pl.when(at.row == at.n_row - 1)
    def _():
        ext[:, :, F + HALF :, :] = jnp.zeros((2, 4, HALF, 128), f32)

    @pl.when(at.col == 0)
    def _():
        ext[:, 0, :, :] = jnp.zeros((2, 2 * F, 128), f32)

    @pl.when(at.col == at.n_col - 1)
    def _():
        ext[:, 3, :, :] = jnp.zeros((2, 2 * F, 128), f32)


def open_kernel(cells, ext, send_sem, recv_sem):
    at = Places()
    meet(at.sides)
    for part in range(2):
        for j in range(2):
            ext[part, 1 + j, TILE, :] = cells[part, :, 128 * j : 128 * j + 128]
    send = Sender(send_sem, recv_sem)
    arrive(halo_first(send, at, ext))
    arrive(halo_second(send, at, ext))
    send.close()
    clear_outside(at, ext)


def step_kernel(last, grad, psum, old, probe, new, probe_new, *scratch):
    acc, rows_in, cols_in, acc0, buf0, acc1, buf1, acc2, buf2, buf3, send_sem, recv_sem = scratch
    at = Places()
    meet((*at.sides, at.twin, *at.along_x, *at.along_y, *at.along_z))
    send = Sender(send_sem, recv_sem)
    above, below = at.row > 0, at.row < at.n_row - 1
    before, after = at.col > 0, at.col < at.n_col - 1
    base = at.core * 128
    base_x = base + at.x * 32
    base_y = base_x + at.y * 8

    s0 = send(psum.at[:, pl.ds(128 - base, 128), :], buf0, at.twin)
    rims = []
    for ch in (0, 2):
        rims.append(send(grad.at[ch, :, ABOVE, :], rows_in.at[ch, 1], at.up))
        rims.append(send(grad.at[ch, :, BELOW, :], rows_in.at[ch, 0], at.down))
    rims.append(send(grad.at[1, 0, :, :], cols_in.at[1, 1], at.left))
    rims.append(send(grad.at[1, 3, :, :], cols_in.at[1, 0], at.right))

    s0.wait_recv()
    acc0[...] = psum[:, pl.ds(base, 128), :] + buf0[...]
    s1 = [
        send(acc0.at[:, pl.ds((at.x + d) % 4 * 32, 32), :], buf1.at[d - 1], at.along_x[d - 1])
        for d in (1, 2, 3)
    ]

    arrive(rims)
    for ch in (0, 2):
        acc[ch, :, BOTTOM, :] = grad[ch, :, BOTTOM, :] + jnp.where(below, rows_in[ch, 1], 0.0)
        acc[ch, :, TOP, :] = grad[ch, :, TOP, :] + jnp.where(above, rows_in[ch, 0], 0.0)
    acc[1, 2, :, :] = grad[1, 2, :, :] + jnp.where(after, cols_in[1, 1], 0.0)
    acc[1, 1, :, :] = grad[1, 1, :, :] + jnp.where(before, cols_in[1, 0], 0.0)
    rims = []
    for ch in (0, 2):
        rims.append(send(acc.at[ch, 0, INNER, :], cols_in.at[ch, 1, INNER, :], at.left))
        rims.append(send(acc.at[ch, 3, INNER, :], cols_in.at[ch, 0, INNER, :], at.right))
    rims.append(send(acc.at[1, BOTH, ABOVE, :], rows_in.at[1, 1, BOTH], at.up))
    rims.append(send(acc.at[1, BOTH, BELOW, :], rows_in.at[1, 0, BOTH], at.down))

    arrive(s1)
    acc1[...] = acc0[:, pl.ds(at.x * 32, 32), :] + buf1[0] + buf1[1] + buf1[2]
    s2 = [
        send(acc1.at[:, pl.ds((at.y + d) % 4 * 8, 8), :], buf2.at[d - 1], at.along_y[d - 1])
        for d in (1, 2, 3)
    ]

    arrive(rims)
    for ch in (0, 2):
        acc[ch, 2, INNER, :] += jnp.where(after, cols_in[ch, 1, INNER, :], 0.0)
        acc[ch, 1, INNER, :] += jnp.where(before, cols_in[ch, 0, INNER, :], 0.0)
    acc[1, BOTH, BOTTOM, :] += jnp.where(below, rows_in[1, 1, BOTH], 0.0)
    acc[1, BOTH, TOP, :] += jnp.where(above, rows_in[1, 0, BOTH], 0.0)
    for j in range(2):
        weight = acc[2, 1 + j, TILE, :] + 1.0
        for part in range(2):
            cells = old[part, 1 + j, TILE, :] - acc[part, 1 + j, TILE, :] / weight
            if last:
                new[part, :, 128 * j : 128 * j + 128] = cells
            else:
                new[part, 1 + j, TILE, :] = cells
    if not last:
        halo = halo_first(send, at, new)

    arrive(s2)
    acc2[...] = acc1[:, pl.ds(at.y * 8, 8), :] + buf2[0] + buf2[1] + buf2[2]
    buf3[at.z] = acc2[...]
    s3 = [send(acc2, buf3.at[at.z], at.along_z[d - 1]) for d in (1, 2, 3)]

    if not last:
        arrive(halo)
        halo = halo_second(send, at, new)

    arrive(s3)
    total = buf3[0] + buf3[1] + buf3[2] + buf3[3]
    mine = pl.ds(base_y, 8)
    probe_new[:, mine, :] = probe[:, mine, :] - total[:2] / (total[2:] + 1.0)
    part = probe_new.at[:, mine, :]
    arrive([send(part, part, peer) for peer in at.along_y])
    part = probe_new.at[:, pl.ds(base_x, 32), :]
    arrive([send(part, part, peer) for peer in at.along_x])
    part = probe_new.at[:, pl.ds(base, 128), :]
    arrive([send(part, part, at.twin)])
    if not last:
        arrive(halo)
    send.close()
    if not last:
        clear_outside(at, new)


VMEM = pl.BlockSpec(memory_space=pltpu.VMEM)
SMEM = pl.BlockSpec(memory_space=pltpu.SMEM)
LIMIT = 48 * 2**20


def open_halo(cells):
    return pl.pallas_call(
        open_kernel,
        out_shape=jax.ShapeDtypeStruct((2, 4, 2 * F, 128), f32),
        in_specs=[VMEM],
        out_specs=VMEM,
        scratch_shapes=[pltpu.SemaphoreType.DMA((8,)), pltpu.SemaphoreType.DMA((8,))],
        compiler_params=pltpu.CompilerParams(
            collective_id=0, has_side_effects=True, vmem_limit_bytes=LIMIT
        ),
    )(cells)


def step(last, grad, psum, old, probe):
    shape = (2, F, F) if last else (2, 4, 2 * F, 128)
    copies = 29 if last else 37
    return pl.pallas_call(
        functools.partial(step_kernel, last),
        out_shape=(jax.ShapeDtypeStruct(shape, f32), jax.ShapeDtypeStruct((2, F, F), f32)),
        in_specs=[VMEM] * 4,
        out_specs=(VMEM, VMEM),
        scratch_shapes=[
            pltpu.VMEM((3, 4, 2 * F, 128), f32),
            pltpu.VMEM((3, 2, 4, HALF, 128), f32),
            pltpu.VMEM((3, 2, 2 * F, 128), f32),
            pltpu.VMEM((3, 128, F), f32),
            pltpu.VMEM((3, 128, F), f32),
            pltpu.VMEM((3, 32, F), f32),
            pltpu.VMEM((3, 3, 32, F), f32),
            pltpu.VMEM((3, 8, F), f32),
            pltpu.VMEM((3, 3, 8, F), f32),
            pltpu.VMEM((4, 3, 8, F), f32),
            pltpu.SemaphoreType.DMA((copies,)),
            pltpu.SemaphoreType.DMA((copies,)),
        ],
        compiler_params=pltpu.CompilerParams(
            collective_id=2 if last else 1, has_side_effects=True, vmem_limit_bytes=LIMIT
        ),
    )(grad, psum, old, probe)


def body(positions, counts, amplitudes, object_field, probe):
    fwd, inv = tables()
    anchor = jnp.stack([lax.axis_index("row") * F - HALF, lax.axis_index("col") * F - HALF])
    corners = positions[0, 0] - anchor[None, :]
    load = counts[0]
    ext = open_halo(object_field)
    for iteration in range(ITERS):
        grad, psum = slots(corners, load, amplitudes[0, 0], ext, probe, fwd, inv)
        ext, probe = step(iteration == ITERS - 1, grad, psum, ext, probe)
    return ext, probe


def solution(mesh):
    return jax.shard_map(
        body,
        mesh=mesh,
        in_specs=(
            P("row", "col", None, None),
            P("row", "col"),
            P("row", "col", None, None, None),
            P(None, "row", "col"),
            P(),
        ),
        out_specs=(P(None, "row", "col"), P()),
        check_vma=False,
    )
```

time: 1290 us -> 218 us (0.17); the launches traced: 1260 us -> 218 us
  waiting for transfers between devices: 322 us -> 0 us
  local copies, waits for them, and re-layouts: 327 us -> 9.8 us
  other arithmetic: 244 us -> 0.08 us
  Pallas kernels: 0 us -> 206 us
  matrix products: 162 us -> 0 us
  loops' own time: 144 us -> 0 us
  starting transfers between devices: 52.9 us -> 0 us
  between operations: 14.5 us -> 1.5 us
    dynamic_update_slice x32 -> x0, local copies, waits for them, and re-layouts: 289 us -> none  [add_patch(): lax.dynamic_update_slice(gradient, present + update, (zero_index, corner_...]
    psum x2 -> x0, waiting for transfers between devices: 270 us -> none  [body(): grad_total, weight_total = lax.psum((probe_sum, weight_sum), ('row', 'col'))]
    pallas_call x0 -> x5, Pallas kernels: none -> 206 us  [the longest x2 114 us: step(): pl.pallas_call(functools.partial(step_kernel, last), out_shape=(jax.Shape...]
    dot_general x128 -> x0, matrix products: 162 us -> none  [complex_product(): jnp.dot(jnp.concatenate([left_re, left_im], 0), jnp.concatenate([right_re...]
    another operation x2 -> x0, loops' own time: 144 us -> none  [body(): lax.fori_loop(0, own_load, own_slot, initial)]
    add x68 -> x0, other arithmetic: 118 us -> none  [the longest x32 61 us: own_slot(): return (gradient, probe_sum + probe_grad, weight_sum + weight)]
    another operation x65 -> x1, other arithmetic: 68.4 us -> 0.08 us  [body(): jnp.stack([lax.axis_index('row') * F - HALF, lax.axis_index('col') * F -...]
    ppermute x16 -> x0, starting transfers between devices: 52.8 us -> none  [the longest x4 31 us: with_halo(): lax.ppermute(tail, axis, [(i, (i + 1) % count) for i in range(ends)])]
  transfers between devices with their start and end apart: 18 -> 0, of which waited for: 13 -> 0; matrix products, arithmetic and copies ran while one was open for 1% -> 0% of each run, Pallas kernels for 0% -> 0%
where the time goes in v1:
time: 218 us
  Pallas kernels  206 us (94%)
  local copies, waits for them, and re-layouts  9.8 us (4%)
    pallas_call x2, Pallas kernels, step(): pl.pallas_call(functools.partial(step_kernel, last), out_shape=(jax.Shape...  114 us
    pallas_call x2, Pallas kernels, slots(): pl.pallas_call(slots_kernel, out_shape=(jax.ShapeDtypeStruct((3, 4, 512,...  63.8 us
    pallas_call x1, Pallas kernels, open_halo(): pl.pallas_call(open_kernel, out_shape=jax.ShapeDtypeStruct((2, 4, 2 * F,...  28.5 us
    unnamed x24, local copies, waits for them, and re-layouts  9.05 us

profile of v1, /device:TPU:1, one launch (start us, length us, event | category | flops | bytes accessed | tf_op | source)
XLA Modules:
  0.0 217.5 jit_solution(15426761238807143983)
XLA Ops:
  0.6 0.0 copy-start.5
  0.6 0.0 copy-start.4
  1.5 0.1 pad_add_fusion
  1.5 0.8 copy.9
  2.3 0.0 copy-start.10
  2.3 1.0 copy-done.10
  3.3 28.5 %shard_map.86.ext.old = f32[2,4,512,128]{3,2,1,0:T(8,128)S(1)} custom-call(f32[2,256,256]{2,1,0:T(8,128)S(1)} %copy-done.10), custom_call_target="tpu_custom_call" | custom-call | tf_op jit(solution)/shard_map/pallas_call | solution.py:291
  31.8 0.0 copy-start
  31.9 1.4 copy-done
  33.2 0.0 copy-done.5
  33.2 0.0 copy-done.4
  33.2 0.0 copy-start.6
  33.2 1.0 copy-done.6
  34.3 0.0 copy-start.8
  34.3 1.0 copy-done.8
  35.3 31.5 %shard_map.87 = (f32[3,4,512,128]{3,2,1,0:T(8,128)}, f32[3,256,256]{2,1,0:T(8,128)S(1)}) custom-call(s32[16,2]{1,0:T(8,128)S(1)} %broadcast_subtract_fusion.corner, s32[1]{0:T(128)} %bitcast.5.load, bf16[16,256,256]{2,1,0:T(8,128)(2,1)S(1)} %bitcast.7, f32[2,4,512,128]{3,2,1,0:T(8,128)} %copy-done, f32[2,256,256]{2,1,0:T(8,128)S(1)} %copy-done.5, ...), custom_call_target="tpu_custom_call" | custom-call | tf_op jit(solution)/shard_map/pallas_call | solution.py:74
  66.8 0.0 copy-start.1
  66.8 1.6 copy-done.1
  68.4 0.0 copy-start.7
  68.4 0.0 copy-start.9
  68.4 61.8 %shard_map.88 = (f32[2,4,512,128]{3,2,1,0:T(8,128)S(1)}, f32[2,256,256]{2,1,0:T(8,128)S(1)}) custom-call(f32[3,4,512,128]{3,2,1,0:T(8,128)} %get-tuple-element.8.grad, f32[3,256,256]{2,1,0:T(8,128)S(1)} %get-tuple-element.9.psum, f32[2,4,512,128]{3,2,1,0:T(8,128)S(1)} %copy-done.1, f32[2,256,256]{2,1,0:T(8,128)S(1)} %copy-done.5), custom_call_target="tpu_custom_call" | custom-call | tf_op jit(solution)/shard_map/pallas_call | solution.py:306
  130.2 0.0 copy-start.2
  130.2 1.4 copy-done.2
  131.5 0.0 copy-done.7
  131.5 0.0 copy-done.9
  131.5 0.0 copy-start.3
  131.5 32.3 %shard_map.89 = (f32[3,4,512,128]{3,2,1,0:T(8,128)}, f32[3,256,256]{2,1,0:T(8,128)S(1)}) custom-call(s32[16,2]{1,0:T(8,128)S(1)} %broadcast_subtract_fusion.corner, s32[1]{0:T(128)} %bitcast.6.load, bf16[16,256,256]{2,1,0:T(8,128)(2,1)S(1)} %bitcast.8, f32[2,4,512,128]{3,2,1,0:T(8,128)} %copy-done.2, f32[2,256,256]{2,1,0:T(8,128)S(1)} %get-tuple-element.11.probe, ...), custom_call_target="tpu_custom_call" | custom-call | tf_op jit(solution)/shard_map/pallas_call | solution.py:74
  163.8 0.0 copy-done.3
  163.9 52.1 %shard_map.90 = (f32[2,256,256]{2,1,0:T(8,128)S(1)}, f32[2,256,256]{2,1,0:T(8,128)S(1)}) custom-call(f32[3,4,512,128]{3,2,1,0:T(8,128)} %get-tuple-element.12.grad, f32[3,256,256]{2,1,0:T(8,128)S(1)} %get-tuple-element.13.psum, f32[2,4,512,128]{3,2,1,0:T(8,128)S(1)} %copy-done.3, f32[2,256,256]{2,1,0:T(8,128)S(1)} %get-tuple-element.11.probe), custom_call_target="tpu_custom_call" | custom-call | tf_op jit(solution)/shard_map/pallas_call | solution.py:306
  215.9 0.8 copy.13
  216.7 0.8 copy.14
  (1 shorter events, 0.0 us)
Async XLA Ops:
  0.6 32.6 %copy-start.5 = (f32[2,256,256]{2,1,0:T(8,128)S(1)}, f32[2,256,256]{2,1,0:T(8,128)}, u32[]{:S(2)}) copy-start(f32[2,256,256]{2,1,0:T(8,128)} %probe.3) | copy-start | bytes 1572868
  0.6 32.6 %copy-start.4 = (bf16[1,1,16,256,256]{4,3,2,1,0:T(8,128)(2,1)S(1)}, bf16[1,1,16,256,256]{4,3,2,1,0:T(8,128)(2,1)}, u32[]{:S(2)}) copy-start(bf16[1,1,16,256,256]{4,3,2,1,0:T(8,128)(2,1)} %param.9) | copy-start | bytes 6291460
  2.3 1.0 copy-start.10
  31.8 1.4 copy-start
  33.2 1.0 copy-start.6
  34.3 1.0 copy-start.8
  66.8 1.6 copy-start.1
  68.4 63.1 %copy-start.7 = (bf16[512,512]{1,0:T(8,128)(2,1)S(1)}, bf16[512,512]{1,0:T(8,128)(2,1)}, u32[]{:S(2)}) copy-start(bf16[512,512]{1,0:T(8,128)(2,1)} %constant.20.clone.inv) | copy-start | bytes 1572868
  68.4 63.1 %copy-start.9 = (bf16[512,512]{1,0:T(8,128)(2,1)S(1)}, bf16[512,512]{1,0:T(8,128)(2,1)}, u32[]{:S(2)}) copy-start(bf16[512,512]{1,0:T(8,128)(2,1)} %constant.19.clone.fwd) | copy-start | bytes 1572868
  130.2 1.4 copy-start.2
  131.5 32.3 %copy-start.3 = (f32[2,4,512,128]{3,2,1,0:T(8,128)S(1)}, f32[2,4,512,128]{3,2,1,0:T(8,128)}, u32[]{:S(2)}) copy-start(f32[2,4,512,128]{3,2,1,0:T(8,128)} %copy-done.2) | copy-start | bytes 6291460

commit v2 on v1

--- a/solution.py
+++ b/solution.py
@@ -26,7 +26,8 @@
     cov[...]=probe[0]*probe[0]+probe[1]*probe[1]
     lane=lax.broadcasted_iota(jnp.int32,(CH,128),1)
     def slot(k,_):
-        r=corner[k,0]; c=corner[k,1]
+        r=corner[0,k]-(lax.axis_index("row")*F-F//2)
+        c=corner[1,k]-(lax.axis_index("col")*F-F//2)
         q=c//128; s=c-q*128
         back=jnp.where(s==0,0,128-s)
         keep=lane<128-s
@@ -76,7 +77,7 @@
         in_specs=[S,S,V,V,V,V,V], out_specs=(V,V),
         scratch_shapes=[pltpu.VMEM((2,F,F),f32),pltpu.VMEM((F,F),f32),pltpu.VMEM((2*F,F),bf16),
             pltpu.VMEM((F,2*F),bf16),pltpu.VMEM((2*F,F),bf16),pltpu.VMEM((F,2*F),f32)],
-        compiler_params=pltpu.CompilerParams(vmem_limit_bytes=48*2**20),
+        compiler_params=pltpu.CompilerParams(vmem_limit_bytes=24*2**20),
     )(corner,load,amp,ext,probe,fwd,inv)
 MESH = pl.DeviceIdType.MESH
 HALF = F // 2
@@ -93,7 +94,12 @@
         self.z = z_hi * 2 + z_lo
         self.up, self.down = ((row + n_row - 1) % n_row, col), ((row + 1) % n_row, col)
         self.left, self.right = (row, (col + n_col - 1) % n_col), (row, (col + 1) % n_col)
-        self.sides = (self.up, self.down, self.left, self.right)
+        north, south = self.up[0], self.down[0]
+        west, east = self.left[1], self.right[1]
+        self.around = (
+            self.up, self.down, self.left, self.right,
+            (north, west), (north, east), (south, west), (south, east),
+        )
         self.twin = (row, col + 1 - 2 * self.core)
         self.along_x = [(row, (self.x + d) % 4 * 4 + col % 4) for d in (1, 2, 3)]
         self.along_y = [(z_lo * 4 + (self.y + d) % 4, col) for d in (1, 2, 3)]
@@ -141,25 +147,27 @@
 
 TOP, BOTTOM = pl.ds(HALF, HALF), pl.ds(F, HALF)
 ABOVE, BELOW = pl.ds(0, HALF), pl.ds(F + HALF, HALF)
-INNER, BOTH, ALL = pl.ds(HALF, F), pl.ds(1, 2), pl.ds(0, 4)
-
-
-def halo_first(send, at, ext):
-    return [
-        send(ext.at[0, BOTH, TOP, :], ext.at[0, BOTH, BELOW, :], at.up),
-        send(ext.at[0, BOTH, BOTTOM, :], ext.at[0, BOTH, ABOVE, :], at.down),
-        send(ext.at[1, 1, INNER, :], ext.at[1, 3, INNER, :], at.left),
-        send(ext.at[1, 2, INNER, :], ext.at[1, 0, INNER, :], at.right),
-    ]
-
-
-def halo_second(send, at, ext):
-    return [
-        send(ext.at[0, 1, :, :], ext.at[0, 3, :, :], at.left),
-        send(ext.at[0, 2, :, :], ext.at[0, 0, :, :], at.right),
-        send(ext.at[1, ALL, TOP, :], ext.at[1, ALL, BELOW, :], at.up),
-        send(ext.at[1, ALL, BOTTOM, :], ext.at[1, ALL, ABOVE, :], at.down),
-    ]
+INNER = pl.ds(HALF, F)
+WEST, EAST = pl.ds(0, 1), pl.ds(3, 1)
+FIRST, SECOND, BOTH = pl.ds(1, 1), pl.ds(2, 1), pl.ds(1, 2)
+OUTSIDE = (
+    (BOTH, ABOVE), (BOTH, BELOW), (WEST, INNER), (EAST, INNER),
+    (WEST, ABOVE), (EAST, ABOVE), (WEST, BELOW), (EAST, BELOW),
+)
+INSIDE = (
+    (BOTH, TOP), (BOTH, BOTTOM), (FIRST, INNER), (SECOND, INNER),
+    (FIRST, TOP), (SECOND, TOP), (FIRST, BOTTOM), (SECOND, BOTTOM),
+)
+OPPOSITE = (1, 0, 3, 2, 7, 6, 5, 4)
+
+
+def send_halo(send, at, ext):
+    copies = []
+    for k, peer in enumerate(at.around):
+        tiles, rows = INSIDE[k]
+        there, below = OUTSIDE[OPPOSITE[k]]
+        copies.append(send(ext.at[:, tiles, rows, :], ext.at[:, there, below, :], peer))
+    return copies
 
 
 def clear_outside(at, ext):
@@ -182,21 +190,20 @@
 
 def open_kernel(cells, ext, send_sem, recv_sem):
     at = Places()
-    meet(at.sides)
+    meet(at.around)
     for part in range(2):
         for j in range(2):
             ext[part, 1 + j, TILE, :] = cells[part, :, 128 * j : 128 * j + 128]
     send = Sender(send_sem, recv_sem)
-    arrive(halo_first(send, at, ext))
-    arrive(halo_second(send, at, ext))
+    arrive(send_halo(send, at, ext))
     send.close()
     clear_outside(at, ext)
 
 
 def step_kernel(last, grad, psum, old, probe, new, probe_new, *scratch):
-    acc, rows_in, cols_in, acc0, buf0, acc1, buf1, acc2, buf2, buf3, send_sem, recv_sem = scratch
+    rims_in, (acc0, buf0, acc1, buf1, acc2, buf2, buf3, send_sem, recv_sem) = scratch[:8], scratch[8:]
     at = Places()
-    meet((*at.sides, at.twin, *at.along_x, *at.along_y, *at.along_z))
+    meet((*at.around, at.twin, *at.along_x, *at.along_y, *at.along_z))
     send = Sender(send_sem, recv_sem)
     above, below = at.row > 0, at.row < at.n_row - 1
     before, after = at.col > 0, at.col < at.n_col - 1
@@ -206,11 +213,9 @@
 
     s0 = send(psum.at[:, pl.ds(128 - base, 128), :], buf0, at.twin)
     rims = []
-    for ch in (0, 2):
-        rims.append(send(grad.at[ch, :, ABOVE, :], rows_in.at[ch, 1], at.up))
-        rims.append(send(grad.at[ch, :, BELOW, :], rows_in.at[ch, 0], at.down))
-    rims.append(send(grad.at[1, 0, :, :], cols_in.at[1, 1], at.left))
-    rims.append(send(grad.at[1, 3, :, :], cols_in.at[1, 0], at.right))
+    for k, peer in enumerate(at.around):
+        tiles, rows = OUTSIDE[k]
+        rims.append(send(grad.at[:, tiles, rows, :], rims_in[OPPOSITE[k]], peer))
 
     s0.wait_recv()
     acc0[...] = psum[:, pl.ds(base, 128), :] + buf0[...]
@@ -218,53 +223,44 @@
         send(acc0.at[:, pl.ds((at.x + d) % 4 * 32, 32), :], buf1.at[d - 1], at.along_x[d - 1])
         for d in (1, 2, 3)
     ]
-
-    arrive(rims)
-    for ch in (0, 2):
-        acc[ch, :, BOTTOM, :] = grad[ch, :, BOTTOM, :] + jnp.where(below, rows_in[ch, 1], 0.0)
-        acc[ch, :, TOP, :] = grad[ch, :, TOP, :] + jnp.where(above, rows_in[ch, 0], 0.0)
-    acc[1, 2, :, :] = grad[1, 2, :, :] + jnp.where(after, cols_in[1, 1], 0.0)
-    acc[1, 1, :, :] = grad[1, 1, :, :] + jnp.where(before, cols_in[1, 0], 0.0)
-    rims = []
-    for ch in (0, 2):
-        rims.append(send(acc.at[ch, 0, INNER, :], cols_in.at[ch, 1, INNER, :], at.left))
-        rims.append(send(acc.at[ch, 3, INNER, :], cols_in.at[ch, 0, INNER, :], at.right))
-    rims.append(send(acc.at[1, BOTH, ABOVE, :], rows_in.at[1, 1, BOTH], at.up))
-    rims.append(send(acc.at[1, BOTH, BELOW, :], rows_in.at[1, 0, BOTH], at.down))
-
     arrive(s1)
     acc1[...] = acc0[:, pl.ds(at.x * 32, 32), :] + buf1[0] + buf1[1] + buf1[2]
     s2 = [
         send(acc1.at[:, pl.ds((at.y + d) % 4 * 8, 8), :], buf2.at[d - 1], at.along_y[d - 1])
         for d in (1, 2, 3)
     ]
-
-    arrive(rims)
-    for ch in (0, 2):
-        acc[ch, 2, INNER, :] += jnp.where(after, cols_in[ch, 1, INNER, :], 0.0)
-        acc[ch, 1, INNER, :] += jnp.where(before, cols_in[ch, 0, INNER, :], 0.0)
-    acc[1, BOTH, BOTTOM, :] += jnp.where(below, rows_in[1, 1, BOTH], 0.0)
-    acc[1, BOTH, TOP, :] += jnp.where(above, rows_in[1, 0, BOTH], 0.0)
-    for j in range(2):
-        weight = acc[2, 1 + j, TILE, :] + 1.0
-        for part in range(2):
-            cells = old[part, 1 + j, TILE, :] - acc[part, 1 + j, TILE, :] / weight
-            if last:
-                new[part, :, 128 * j : 128 * j + 128] = cells
-            else:
-                new[part, 1 + j, TILE, :] = cells
-    if not last:
-        halo = halo_first(send, at, new)
-
     arrive(s2)
     acc2[...] = acc1[:, pl.ds(at.y * 8, 8), :] + buf2[0] + buf2[1] + buf2[2]
     buf3[at.z] = acc2[...]
     s3 = [send(acc2, buf3.at[at.z], at.along_z[d - 1]) for d in (1, 2, 3)]
 
+    def finish_object():
+        arrive(rims)
+        for j, (side, near) in enumerate(((before, 2), (after, 3))):
+            for half, (level, over, corner) in enumerate(
+                ((above, 0, 4 + j), (below, 1, 6 + j))
+            ):
+                rows = pl.ds(HALF * half, HALF)
+                sums = []
+                for ch in range(3):
+                    sums.append(
+                        grad[ch, 1 + j, pl.ds(HALF + HALF * half, HALF), :]
+                        + jnp.where(level, rims_in[over][ch, j], 0.0)
+                        + jnp.where(side, rims_in[near][ch, 0, rows, :], 0.0)
+                        + jnp.where(side & level, rims_in[corner][ch, 0], 0.0)
+                    )
+                weight = sums[2] + 1.0
+                for part in range(2):
+                    place = pl.ds(HALF + HALF * half, HALF)
+                    cells = old[part, 1 + j, place, :] - sums[part] / weight
+                    if last:
+                        new[part, rows, 128 * j : 128 * j + 128] = cells
+                    else:
+                        new[part, 1 + j, place, :] = cells
+
     if not last:
-        arrive(halo)
-        halo = halo_second(send, at, new)
-
+        finish_object()
+        halo = send_halo(send, at, new)
     arrive(s3)
     total = buf3[0] + buf3[1] + buf3[2] + buf3[3]
     mine = pl.ds(base_y, 8)
@@ -272,7 +268,10 @@
     part = probe_new.at[:, mine, :]
     arrive([send(part, part, peer) for peer in at.along_y])
     part = probe_new.at[:, pl.ds(base_x, 32), :]
-    arrive([send(part, part, peer) for peer in at.along_x])
+    s5 = [send(part, part, peer) for peer in at.along_x]
+    if last:
+        finish_object()
+    arrive(s5)
     part = probe_new.at[:, pl.ds(base, 128), :]
     arrive([send(part, part, at.twin)])
     if not last:
@@ -284,7 +283,7 @@
 
 VMEM = pl.BlockSpec(memory_space=pltpu.VMEM)
 SMEM = pl.BlockSpec(memory_space=pltpu.SMEM)
-LIMIT = 48 * 2**20
+LIMIT = 20 * 2**20
 
 
 def open_halo(cells):
@@ -302,16 +301,16 @@
 
 def step(last, grad, psum, old, probe):
     shape = (2, F, F) if last else (2, 4, 2 * F, 128)
-    copies = 29 if last else 37
+    copies = 25 if last else 33
     return pl.pallas_call(
         functools.partial(step_kernel, last),
         out_shape=(jax.ShapeDtypeStruct(shape, f32), jax.ShapeDtypeStruct((2, F, F), f32)),
         in_specs=[VMEM] * 4,
         out_specs=(VMEM, VMEM),
         scratch_shapes=[
-            pltpu.VMEM((3, 4, 2 * F, 128), f32),
-            pltpu.VMEM((3, 2, 4, HALF, 128), f32),
-            pltpu.VMEM((3, 2, 2 * F, 128), f32),
+            *(pltpu.VMEM((3, 2, HALF, 128), f32) for _ in range(2)),
+            *(pltpu.VMEM((3, 1, F, 128), f32) for _ in range(2)),
+            *(pltpu.VMEM((3, 1, HALF, 128), f32) for _ in range(4)),
             pltpu.VMEM((3, 128, F), f32),
             pltpu.VMEM((3, 128, F), f32),
             pltpu.VMEM((3, 32, F), f32),
@@ -330,8 +329,7 @@
 
 def body(positions, counts, amplitudes, object_field, probe):
     fwd, inv = tables()
-    anchor = jnp.stack([lax.axis_index("row") * F - HALF, lax.axis_index("col") * F - HALF])
-    corners = positions[0, 0] - anchor[None, :]
+    corners = positions[0, 0].T
     load = counts[0]
     ext = open_halo(object_field)
     for iteration in range(ITERS):

time: 218 us -> 197 us (0.904)
  Pallas kernels: 206 us -> 191 us
  local copies, waits for them, and re-layouts: 9.8 us -> 4.73 us
    pallas_call x2, Pallas kernels: 63.8 us -> 9.2 us  [slots(): pl.pallas_call(slots_kernel, out_shape=(jax.ShapeDtypeStruct((3, 4, 512,...]
    pallas_call x2, Pallas kernels: 114 us -> 155 us  [step(): pl.pallas_call(functools.partial(step_kernel, last), out_shape=(jax.Shape...]
    unnamed x24 -> x18, local copies, waits for them, and re-layouts: 9.05 us -> 4.73 us
where the time goes in v2:
time: 197 us
  Pallas kernels  191 us (97%)
  local copies, waits for them, and re-layouts  4.73 us (2%)
    pallas_call x2, Pallas kernels, step(): pl.pallas_call(functools.partial(step_kernel, last), out_shape=(jax.Shape...  155 us
    pallas_call x1, Pallas kernels, open_halo(): pl.pallas_call(open_kernel, out_shape=jax.ShapeDtypeStruct((2, 4, 2 * F,...  26.5 us
    pallas_call x2, Pallas kernels, slots(): pl.pallas_call(slots_kernel, out_shape=(jax.ShapeDtypeStruct((3, 4, 512,...  9.2 us
    unnamed x18, local copies, waits for them, and re-layouts  4.73 us

profile of v2, /device:TPU:1, one launch (start us, length us, event | category | flops | bytes accessed | tf_op | source)
XLA Modules:
  0.0 197.0 jit_solution(17568100415909818616)
XLA Ops:
  0.6 0.0 copy-start.1
  0.6 0.0 copy-start
  1.4 0.0 copy-start.6
  1.5 1.0 copy-done.6
  2.5 0.0 copy-start.7
  2.5 26.5 %shard_map.86.ext.old = f32[2,4,512,128]{3,2,1,0:T(8,128)S(1)} custom-call(f32[2,256,256]{2,1,0:T(8,128)S(1)} %copy-done.6), custom_call_target="tpu_custom_call" | custom-call | tf_op jit(solution)/shard_map/pallas_call | solution.py:290
  29.0 0.0 copy-done.1
  29.0 0.0 copy-done
  29.0 0.0 copy-done.7
  29.0 0.0 copy-start.2
  29.1 1.0 copy-done.2
  30.1 0.0 copy-start.4
  30.1 1.0 copy-done.4
  31.1 4.6 %shard_map.87 = (f32[3,4,512,128]{3,2,1,0:T(8,128)S(1)}, f32[3,256,256]{2,1,0:T(8,128)S(1)}) custom-call(s32[2,16]{1,0:T(2,128)S(1)} %bitcast.9, s32[1]{0:T(128)} %bitcast.5.load, bf16[16,256,256]{2,1,0:T(8,128)(2,1)S(1)} %bitcast.7, f32[2,4,512,128]{3,2,1,0:T(8,128)S(1)} %shard_map.86.ext.old, f32[2,256,256]{2,1,0:T(8,128)S(1)} %copy-done.1, ...), custom_call_target="tpu_custom_call" | custom-call | tf_op jit(solution)/shard_map/pallas_call | solution.py:75
  35.8 0.0 copy-start.3
  35.8 0.0 copy-start.5
  35.8 80.7 %shard_map.88 = (f32[2,4,512,128]{3,2,1,0:T(8,128)S(1)}, f32[2,256,256]{2,1,0:T(8,128)S(1)}) custom-call(f32[3,4,512,128]{3,2,1,0:T(8,128)S(1)} %get-tuple-element.8.grad, f32[3,256,256]{2,1,0:T(8,128)S(1)} %get-tuple-element.9.psum, f32[2,4,512,128]{3,2,1,0:T(8,128)S(1)} %shard_map.86.ext.old, f32[2,256,256]{2,1,0:T(8,128)S(1)} %copy-done.1), custom_call_target="tpu_custom_call" | custom-call | tf_op jit(solution)/shard_map/pallas_call | solution.py:305
  116.5 0.0 copy-done.3
  116.6 0.0 copy-done.5
  116.6 4.6 %shard_map.89 = (f32[3,4,512,128]{3,2,1,0:T(8,128)S(1)}, f32[3,256,256]{2,1,0:T(8,128)S(1)}) custom-call(s32[2,16]{1,0:T(2,128)S(1)} %bitcast.10, s32[1]{0:T(128)} %bitcast.6.load, bf16[16,256,256]{2,1,0:T(8,128)(2,1)S(1)} %bitcast.8, f32[2,4,512,128]{3,2,1,0:T(8,128)S(1)} %get-tuple-element.10.ext.old, f32[2,256,256]{2,1,0:T(8,128)S(1)} %get-tuple-element.11.probe, ...), custom_call_target="tpu_custom_call" | custom-call | tf_op jit(solution)/shard_map/pallas_call | solution.py:75
  121.1 74.2 %shard_map.90 = (f32[2,256,256]{2,1,0:T(8,128)S(1)}, f32[2,256,256]{2,1,0:T(8,128)S(1)}) custom-call(f32[3,4,512,128]{3,2,1,0:T(8,128)S(1)} %get-tuple-element.12.grad, f32[3,256,256]{2,1,0:T(8,128)S(1)} %get-tuple-element.13.psum, f32[2,4,512,128]{3,2,1,0:T(8,128)S(1)} %get-tuple-element.10.ext.old, f32[2,256,256]{2,1,0:T(8,128)S(1)} %get-tuple-element.11.probe), custom_call_target="tpu_custom_call" | custom-call | tf_op jit(solution)/shard_map/pallas_call | solution.py:305
  195.4 0.8 copy.12
  196.2 0.8 copy.13
Async XLA Ops:
  0.6 28.4 %copy-start.1 = (f32[2,256,256]{2,1,0:T(8,128)S(1)}, f32[2,256,256]{2,1,0:T(8,128)}, u32[]{:S(2)}) copy-start(f32[2,256,256]{2,1,0:T(8,128)} %probe.3) | copy-start | bytes 1572868
  0.6 28.4 %copy-start = (bf16[1,1,16,256,256]{4,3,2,1,0:T(8,128)(2,1)S(1)}, bf16[1,1,16,256,256]{4,3,2,1,0:T(8,128)(2,1)}, u32[]{:S(2)}) copy-start(bf16[1,1,16,256,256]{4,3,2,1,0:T(8,128)(2,1)} %param.9) | copy-start | bytes 6291460
  1.4 1.0 copy-start.6
  2.5 26.5 %copy-start.7 = (s32[1,1,16,2]{2,3,1,0:T(2,128)S(1)}, s32[1,1,16,2]{2,3,1,0:T(2,128)}, u32[]{:S(2)}) copy-start(s32[1,1,16,2]{2,3,1,0:T(2,128)} %param.7) | copy-start | bytes 388
  29.0 1.0 copy-start.2
  30.1 1.0 copy-start.4
  35.8 80.8 %copy-start.3 = (bf16[512,512]{1,0:T(8,128)(2,1)S(1)}, bf16[512,512]{1,0:T(8,128)(2,1)}, u32[]{:S(2)}) copy-start(bf16[512,512]{1,0:T(8,128)(2,1)} %constant.5.clone.inv) | copy-start | bytes 1572868
  35.8 80.8 %copy-start.5 = (bf16[512,512]{1,0:T(8,128)(2,1)S(1)}, bf16[512,512]{1,0:T(8,128)(2,1)}, u32[]{:S(2)}) copy-start(bf16[512,512]{1,0:T(8,128)(2,1)} %constant.4.clone.fwd) | copy-start | bytes 1572868

commit v3 on v2

--- a/solution.py
+++ b/solution.py
@@ -18,67 +18,101 @@
     fwd=np.block([[re,-im],[im,re]]); inv=np.block([[re,im],[-im,re]])
     return jnp.asarray(fwd,bf16), jnp.asarray(inv,bf16)
 
-CH=16
+CH=16; B=2; ROWS=3*F
+def both_sides(table, other, cells):
+    re = jnp.dot(table[:F, :], cells[...], preferred_element_type=f32).astype(bf16)
+    im = jnp.dot(table[F:, :], cells[...], preferred_element_type=f32).astype(bf16)
+    stacked = jnp.concatenate(
+        [jnp.concatenate([re[:, F * b : F * b + F], im[:, F * b : F * b + F]], 1) for b in range(B)], 0
+    )
+    return jnp.dot(stacked, other[...], preferred_element_type=f32)
+
+
 def slots_kernel(corner, load, amp, ext, probe, fwd, inv, grad, psum,
-                 patch, cov, exit_s, half_s, miss_s, chi_s):
-    grad[...]=jnp.zeros(grad.shape,f32)
+                 patch0, patch1, cov, exit_s, miss0, miss1, chi_s):
+    lane=lax.broadcasted_iota(jnp.int32,(CH,128),1)
+    n=load[0]
+    top=lax.axis_index("row")*F-F//2; left=lax.axis_index("col")*F-F//2
+    def place(k):
+        kk=jnp.minimum(k,15)
+        live=k<n
+        r=jnp.where(live,corner[0,kk]-top,2*F); c=jnp.where(live,corner[1,kk]-left,0)
+        q=c//128; s=c-q*128
+        return r,q,s,kk
+    def front(g,patch,miss):
+        for b in range(B):
+            r,q,s,kk=place(B*g+b)
+            back=jnp.where(s==0,0,128-s)
+            keep=lane<128-s
+            for i in range(F//CH):
+                rows=pl.ds(i*CH,CH)
+                got=[]
+                for ch in range(2):
+                    t=[pltpu.roll(ext[ch,q+j,pl.ds(r+i*CH,CH),:],back,1) for j in range(3)]
+                    got.append(jnp.concatenate([jnp.where(keep,t[0],t[1]),jnp.where(keep,t[1],t[2])],1))
+                re,im=got
+                patch[b,0,rows,:]=re; patch[b,1,rows,:]=im
+                pr=probe[0,rows,:]; pi=probe[1,rows,:]
+                exit_s[rows,F*b:F*b+F]=(pr*re-pi*im).astype(bf16)
+                exit_s[pl.ds(F+i*CH,CH),F*b:F*b+F]=(pr*im+pi*re).astype(bf16)
+        far=both_sides(fwd,inv,exit_s)
+        for b in range(B):
+            kk=jnp.minimum(B*g+b,15)
+            fr=far[F*b:F*b+F,:F]; fi=far[F*b:F*b+F,F:]
+            ratio=1.0-amp[kk].astype(f32)*lax.rsqrt(fr*fr+fi*fi+1.0)
+            miss[:F,F*b:F*b+F]=(fr*ratio).astype(bf16)
+            miss[F:,F*b:F*b+F]=(fi*ratio).astype(bf16)
+    def back_(g,patch,miss):
+        chi=both_sides(inv,fwd,miss)
+        chi_s[...]=chi
+        for i in range(F//CH):
+            rows=pl.ds(i*CH,CH)
+            pr=probe[0,rows,:]; pi=probe[1,rows,:]
+            p0=p1=p2=0.0
+            for b in range(B):
+                at_=pl.ds(F*b+i*CH,CH)
+                cr=chi_s[at_,:F]; ci=chi_s[at_,F:]
+                re=patch[b,0,rows,:]; im=patch[b,1,rows,:]
+                p0+=re*cr+im*ci; p1+=re*ci-im*cr; p2+=re*re+im*im
+            psum[0,rows,:]+=p0; psum[1,rows,:]+=p1; psum[2,rows,:]+=p2
+        for b in range(B):
+            r,q,s,kk=place(B*g+b)
+            put=lane>=s
+            for i in range(F//CH):
+                rows=pl.ds(i*CH,CH); at_=pl.ds(F*b+i*CH,CH)
+                cr=chi_s[at_,:F]; ci=chi_s[at_,F:]
+                pr=probe[0,rows,:]; pi=probe[1,rows,:]
+                for ch,u in ((0,pr*cr+pi*ci),(1,pr*ci-pi*cr),(2,cov[rows,:])):
+                    u0=pltpu.roll(u[:,:128],s,1); u1=pltpu.roll(u[:,128:],s,1)
+                    at=pl.ds(r+i*CH,CH)
+                    grad[ch,q,at,:]+=jnp.where(put,u0,0.0)
+                    grad[ch,q+1,at,:]+=jnp.where(put,u1,u0)
+                    grad[ch,q+2,at,:]+=jnp.where(put,0.0,u1)
+    for ch in range(3):
+        for j in range(4):
+            grad[ch,j,:2*F,:]=jnp.zeros((2*F,128),f32)
     psum[...]=jnp.zeros(psum.shape,f32)
     cov[...]=probe[0]*probe[0]+probe[1]*probe[1]
-    lane=lax.broadcasted_iota(jnp.int32,(CH,128),1)
-    def slot(k,_):
-        r=corner[0,k]-(lax.axis_index("row")*F-F//2)
-        c=corner[1,k]-(lax.axis_index("col")*F-F//2)
-        q=c//128; s=c-q*128
-        back=jnp.where(s==0,0,128-s)
-        keep=lane<128-s
-        for i in range(F//CH):
-            rows=pl.ds(i*CH,CH)
-            got=[]
-            for ch in range(2):
-                t=[pltpu.roll(ext[ch,q+j,pl.ds(r+i*CH,CH),:],back,1) for j in range(3)]
-                got.append(jnp.concatenate([jnp.where(keep,t[0],t[1]),jnp.where(keep,t[1],t[2])],1))
-            re,im=got
-            patch[0,rows,:]=re; patch[1,rows,:]=im
-            pr=probe[0,rows,:]; pi=probe[1,rows,:]
-            exit_s[rows,:]=(pr*re-pi*im).astype(bf16)
-            exit_s[pl.ds(F+i*CH,CH),:]=(pr*im+pi*re).astype(bf16)
-            psum[2,rows,:]+=re*re+im*im
-        half=jnp.dot(fwd[...],exit_s[...],preferred_element_type=f32).astype(bf16)
-        half_s[:,:F]=half[:F]; half_s[:,F:]=half[F:]
-        far=jnp.dot(half_s[...],inv[...],preferred_element_type=f32)
-        fr=far[:,:F]; fi=far[:,F:]
-        ratio=1.0-amp[k].astype(f32)*lax.rsqrt(fr*fr+fi*fi+1.0)
-        miss_s[:F,:]=(fr*ratio).astype(bf16)
-        miss_s[F:,:]=(fi*ratio).astype(bf16)
-        back_=jnp.dot(inv[...],miss_s[...],preferred_element_type=f32).astype(bf16)
-        half_s[:,:F]=back_[:F]; half_s[:,F:]=back_[F:]
-        chi_s[...]=jnp.dot(half_s[...],fwd[...],preferred_element_type=f32)
-        put=lane>=s
-        for i in range(F//CH):
-            rows=pl.ds(i*CH,CH)
-            cr=chi_s[rows,:F]; ci=chi_s[rows,F:]
-            pr=probe[0,rows,:]; pi=probe[1,rows,:]
-            re=patch[0,rows,:]; im=patch[1,rows,:]
-            psum[0,rows,:]+=re*cr+im*ci
-            psum[1,rows,:]+=re*ci-im*cr
-            for ch,u in ((0,pr*cr+pi*ci),(1,pr*ci-pi*cr),(2,cov[rows,:])):
-                u0=pltpu.roll(u[:,:128],s,1); u1=pltpu.roll(u[:,128:],s,1)
-                at=pl.ds(r+i*CH,CH)
-                grad[ch,q,at,:]+=jnp.where(put,u0,0.0)
-                grad[ch,q+1,at,:]+=jnp.where(put,u1,u0)
-                grad[ch,q+2,at,:]+=jnp.where(put,0.0,u1)
+    front(0,patch0,miss0)
+    pairs=(n+2*B-1)//(2*B)
+    def it(j,_):
+        back_(2*j,patch0,miss0)
+        front(2*j+1,patch1,miss1)
+        back_(2*j+1,patch1,miss1)
+        front(2*j+2,patch0,miss0)
         return 0
-    lax.fori_loop(0,load[0],slot,0)
-
+    lax.fori_loop(0,pairs,it,0)
 def slots(corner,load,amp,ext,probe,fwd,inv):
     V=pl.BlockSpec(memory_space=pltpu.VMEM); S=pl.BlockSpec(memory_space=pltpu.SMEM)
     return pl.pallas_call(slots_kernel,
-        out_shape=(jax.ShapeDtypeStruct((3,4,512,128),f32),jax.ShapeDtypeStruct((3,F,F),f32)),
+        out_shape=(jax.ShapeDtypeStruct((3,4,ROWS,128),f32),jax.ShapeDtypeStruct((3,F,F),f32)),
         in_specs=[S,S,V,V,V,V,V], out_specs=(V,V),
-        scratch_shapes=[pltpu.VMEM((2,F,F),f32),pltpu.VMEM((F,F),f32),pltpu.VMEM((2*F,F),bf16),
-            pltpu.VMEM((F,2*F),bf16),pltpu.VMEM((2*F,F),bf16),pltpu.VMEM((F,2*F),f32)],
+        scratch_shapes=[pltpu.VMEM((B,2,F,F),f32),pltpu.VMEM((B,2,F,F),f32),pltpu.VMEM((F,F),f32),pltpu.VMEM((2*F,B*F),bf16),
+            pltpu.VMEM((2*F,B*F),bf16),pltpu.VMEM((2*F,B*F),bf16),pltpu.VMEM((B*F,2*F),f32)],
         compiler_params=pltpu.CompilerParams(vmem_limit_bytes=24*2**20),
     )(corner,load,amp,ext,probe,fwd,inv)
+
+
 MESH = pl.DeviceIdType.MESH
 HALF = F // 2
 TILE = slice(HALF, HALF + F)
@@ -171,21 +205,23 @@
 
 
 def clear_outside(at, ext):
+    ext[:, :, 2 * F :, :] = jnp.zeros((2, 4, ROWS - 2 * F, 128), f32)
+
     @pl.when(at.row == 0)
     def _():
         ext[:, :, :HALF, :] = jnp.zeros((2, 4, HALF, 128), f32)
 
     @pl.when(at.row == at.n_row - 1)
     def _():
-        ext[:, :, F + HALF :, :] = jnp.zeros((2, 4, HALF, 128), f32)
+        ext[:, :, F + HALF : 2 * F, :] = jnp.zeros((2, 4, HALF, 128), f32)
 
     @pl.when(at.col == 0)
     def _():
-        ext[:, 0, :, :] = jnp.zeros((2, 2 * F, 128), f32)
+        ext[:, 0, : 2 * F, :] = jnp.zeros((2, 2 * F, 128), f32)
 
     @pl.when(at.col == at.n_col - 1)
     def _():
-        ext[:, 3, :, :] = jnp.zeros((2, 2 * F, 128), f32)
+        ext[:, 3, : 2 * F, :] = jnp.zeros((2, 2 * F, 128), f32)
 
 
 def open_kernel(cells, ext, send_sem, recv_sem):
@@ -289,7 +325,7 @@
 def open_halo(cells):
     return pl.pallas_call(
         open_kernel,
-        out_shape=jax.ShapeDtypeStruct((2, 4, 2 * F, 128), f32),
+        out_shape=jax.ShapeDtypeStruct((2, 4, ROWS, 128), f32),
         in_specs=[VMEM],
         out_specs=VMEM,
         scratch_shapes=[pltpu.SemaphoreType.DMA((8,)), pltpu.SemaphoreType.DMA((8,))],
@@ -300,7 +336,7 @@
 
 
 def step(last, grad, psum, old, probe):
-    shape = (2, F, F) if last else (2, 4, 2 * F, 128)
+    shape = (2, F, F) if last else (2, 4, ROWS, 128)
     copies = 25 if last else 33
     return pl.pallas_call(
         functools.partial(step_kernel, last),

time: 197 us -> 169 us (0.86)
  Pallas kernels: 191 us -> 165 us
    pallas_call x2, Pallas kernels: 155 us -> 127 us  [step(): pl.pallas_call(functools.partial(step_kernel, last), out_shape=(jax.Shape...]
    pallas_call x3, Pallas kernels: 35.7 us -> 37.9 us  [the longest x1 26.6 us: open_halo(): pl.pallas_call(open_kernel, out_shape=jax.ShapeDtypeStruct((2, 4, ROWS, 1...]
    unnamed x18 -> x14, local copies, waits for them, and re-layouts: 4.73 us -> 2.93 us
where the time goes in v3:
time: 169 us
  Pallas kernels  165 us (98%)
  local copies, waits for them, and re-layouts  2.93 us (2%)
    pallas_call x2, Pallas kernels, step(): pl.pallas_call(functools.partial(step_kernel, last), out_shape=(jax.Shape...  127 us
    pallas_call x1, Pallas kernels, open_halo(): pl.pallas_call(open_kernel, out_shape=jax.ShapeDtypeStruct((2, 4, ROWS, 1...  26.6 us
    pallas_call x2, Pallas kernels, slots(): pl.pallas_call(slots_kernel, out_shape=(jax.ShapeDtypeStruct((3, 4, ROWS,...  11.3 us

profile of v3, /device:TPU:1, one launch (start us, length us, event | category | flops | bytes accessed | tf_op | source)
XLA Modules:
  0.0 169.4 jit_solution(11529264090615181886)
XLA Ops:
  0.6 0.0 copy-start.2
  0.6 0.0 copy-start.3
  0.7 0.0 copy-start.1
  0.7 0.0 copy-start
  1.5 0.0 copy-start.4
  1.5 1.3 copy-done.4
  2.8 0.0 copy-start.5
  2.8 26.6 %shard_map.86.ext.old = f32[2,4,768,128]{3,2,1,0:T(8,128)S(1)} custom-call(f32[2,256,256]{2,1,0:T(8,128)S(1)} %copy-done.4), custom_call_target="tpu_custom_call" | custom-call | tf_op jit(solution)/shard_map/pallas_call | solution.py:326
  29.4 0.0 copy-done.2
  29.4 0.0 copy-done.3
  29.4 0.0 copy-done.1
  29.4 0.0 copy-done
  29.4 0.0 copy-done.5
  29.4 5.7 %shard_map.87 = (f32[3,4,768,128]{3,2,1,0:T(8,128)S(1)}, f32[3,256,256]{2,1,0:T(8,128)S(1)}) custom-call(s32[2,16]{1,0:T(2,128)S(1)} %bitcast.9, s32[1]{0:T(128)} %bitcast.5.load, bf16[16,256,256]{2,1,0:T(8,128)(2,1)S(1)} %bitcast.7, f32[2,4,768,128]{3,2,1,0:T(8,128)S(1)} %shard_map.86.ext.old, f32[2,256,256]{2,1,0:T(8,128)S(1)} %copy-done.1, ...), custom_call_target="tpu_custom_call" | custom-call | tf_op jit(solution)/shard_map/pallas_call | solution.py:107
  35.1 67.7 %shard_map.88 = (f32[2,4,768,128]{3,2,1,0:T(8,128)S(1)}, f32[2,256,256]{2,1,0:T(8,128)S(1)}) custom-call(f32[3,4,768,128]{3,2,1,0:T(8,128)S(1)} %get-tuple-element.8.grad, f32[3,256,256]{2,1,0:T(8,128)S(1)} %get-tuple-element.9.psum, f32[2,4,768,128]{3,2,1,0:T(8,128)S(1)} %shard_map.86.ext.old, f32[2,256,256]{2,1,0:T(8,128)S(1)} %copy-done.1), custom_call_target="tpu_custom_call" | custom-call | tf_op jit(solution)/shard_map/pallas_call | solution.py:341
  102.8 5.7 %shard_map.89 = (f32[3,4,768,128]{3,2,1,0:T(8,128)S(1)}, f32[3,256,256]{2,1,0:T(8,128)S(1)}) custom-call(s32[2,16]{1,0:T(2,128)S(1)} %bitcast.10, s32[1]{0:T(128)} %bitcast.6.load, bf16[16,256,256]{2,1,0:T(8,128)(2,1)S(1)} %bitcast.8, f32[2,4,768,128]{3,2,1,0:T(8,128)S(1)} %get-tuple-element.10.ext.old, f32[2,256,256]{2,1,0:T(8,128)S(1)} %get-tuple-element.11.probe, ...), custom_call_target="tpu_custom_call" | custom-call | tf_op jit(solution)/shard_map/pallas_call | solution.py:107
  108.5 59.3 %shard_map.90 = (f32[2,256,256]{2,1,0:T(8,128)S(1)}, f32[2,256,256]{2,1,0:T(8,128)S(1)}) custom-call(f32[3,4,768,128]{3,2,1,0:T(8,128)S(1)} %get-tuple-element.12.grad, f32[3,256,256]{2,1,0:T(8,128)S(1)} %get-tuple-element.13.psum, f32[2,4,768,128]{3,2,1,0:T(8,128)S(1)} %get-tuple-element.10.ext.old, f32[2,256,256]{2,1,0:T(8,128)S(1)} %get-tuple-element.11.probe), custom_call_target="tpu_custom_call" | custom-call | tf_op jit(solution)/shard_map/pallas_call | solution.py:341
  167.8 0.8 copy.12
  168.6 0.8 copy.13
Async XLA Ops:
  0.6 28.8 %copy-start.2 = (bf16[512,512]{1,0:T(8,128)(2,1)S(1)}, bf16[512,512]{1,0:T(8,128)(2,1)}, u32[]{:S(2)}) copy-start(bf16[512,512]{1,0:T(8,128)(2,1)} %constant.5.clone.inv) | copy-start | bytes 1572868
  0.6 28.8 %copy-start.3 = (bf16[512,512]{1,0:T(8,128)(2,1)S(1)}, bf16[512,512]{1,0:T(8,128)(2,1)}, u32[]{:S(2)}) copy-start(bf16[512,512]{1,0:T(8,128)(2,1)} %constant.4.clone.fwd) | copy-start | bytes 1572868
  0.7 28.8 %copy-start.1 = (f32[2,256,256]{2,1,0:T(8,128)S(1)}, f32[2,256,256]{2,1,0:T(8,128)}, u32[]{:S(2)}) copy-start(f32[2,256,256]{2,1,0:T(8,128)} %probe.3) | copy-start | bytes 1572868
  0.7 28.8 %copy-start = (bf16[1,1,16,256,256]{4,3,2,1,0:T(8,128)(2,1)S(1)}, bf16[1,1,16,256,256]{4,3,2,1,0:T(8,128)(2,1)}, u32[]{:S(2)}) copy-start(bf16[1,1,16,256,256]{4,3,2,1,0:T(8,128)(2,1)} %param.9) | copy-start | bytes 6291460
  1.5 1.3 copy-start.4
  2.8 26.6 %copy-start.5 = (s32[1,1,16,2]{2,3,1,0:T(2,128)S(1)}, s32[1,1,16,2]{2,3,1,0:T(2,128)}, u32[]{:S(2)}) copy-start(s32[1,1,16,2]{2,3,1,0:T(2,128)} %param.7) | copy-start | bytes 388

commit v4 on v3

--- a/solution.py
+++ b/solution.py
@@ -118,6 +118,10 @@
 TILE = slice(HALF, HALF + F)
 
 
+TOP, BOTTOM = pl.ds(HALF, HALF), pl.ds(F, HALF)
+ABOVE, BELOW = pl.ds(0, HALF), pl.ds(F + HALF, HALF)
+
+
 class Places:
     def __init__(self):
         row, col = lax.axis_index("row"), lax.axis_index("col")
@@ -135,6 +139,16 @@
             (north, west), (north, east), (south, west), (south, east),
         )
         self.twin = (row, col + 1 - 2 * self.core)
+        beside = (col + n_col - 1 + 2 * self.core) % n_col
+        inner, outer = 3 - 3 * self.core, 3 * self.core
+        self.near_corners = (
+            ((north, self.twin[1]), ABOVE, inner, 2 + self.core),
+            ((south, self.twin[1]), BELOW, inner, self.core),
+        )
+        self.far_corners = (
+            ((north, beside), ABOVE, outer, 3 - self.core),
+            ((south, beside), BELOW, outer, 1 - self.core),
+        )
         self.along_x = [(row, (self.x + d) % 4 * 4 + col % 4) for d in (1, 2, 3)]
         self.along_y = [(z_lo * 4 + (self.y + d) % 4, col) for d in (1, 2, 3)]
         self.along_z = []
@@ -179,8 +193,6 @@
         copy.wait_recv()
 
 
-TOP, BOTTOM = pl.ds(HALF, HALF), pl.ds(F, HALF)
-ABOVE, BELOW = pl.ds(0, HALF), pl.ds(F + HALF, HALF)
 INNER = pl.ds(HALF, F)
 WEST, EAST = pl.ds(0, 1), pl.ds(3, 1)
 FIRST, SECOND, BOTH = pl.ds(1, 1), pl.ds(2, 1), pl.ds(1, 2)
@@ -237,44 +249,56 @@
 
 
 def step_kernel(last, grad, psum, old, probe, new, probe_new, *scratch):
-    rims_in, (acc0, buf0, acc1, buf1, acc2, buf2, buf3, send_sem, recv_sem) = scratch[:8], scratch[8:]
+    rims_in, corners_in = scratch[:4], scratch[4]
+    acc0, buf0, acc1, buf1, acc2, buf2, buf3, send_sem, recv_sem = scratch[5:]
     at = Places()
     meet((*at.around, at.twin, *at.along_x, *at.along_y, *at.along_z))
     send = Sender(send_sem, recv_sem)
     above, below = at.row > 0, at.row < at.n_row - 1
     before, after = at.col > 0, at.col < at.n_col - 1
     base = at.core * 128
-    base_x = base + at.x * 32
-    base_y = base_x + at.y * 8
+    base_y = base + at.y * 32
+    base_x = base_y + at.x * 8
+    rims = []
+
+    def send_rims(channels, sides):
+        for k in sides:
+            tiles, rows = OUTSIDE[k]
+            there = rims_in[OPPOSITE[k]].at[channels]
+            rims.append(send(grad.at[channels, tiles, rows, :], there, at.around[k]))
+
+    def send_corners(corners):
+        for peer, rows, tile, there in corners:
+            rims.append(send(grad.at[:, pl.ds(tile, 1), rows, :], corners_in.at[there], peer))
 
     s0 = send(psum.at[:, pl.ds(128 - base, 128), :], buf0, at.twin)
-    rims = []
-    for k, peer in enumerate(at.around):
-        tiles, rows = OUTSIDE[k]
-        rims.append(send(grad.at[:, tiles, rows, :], rims_in[OPPOSITE[k]], peer))
-
+    send_rims(pl.ds(0, 1), (0, 1))
+    send_rims(pl.ds(0, 3), (2, 3))
     s0.wait_recv()
     acc0[...] = psum[:, pl.ds(base, 128), :] + buf0[...]
     s1 = [
-        send(acc0.at[:, pl.ds((at.x + d) % 4 * 32, 32), :], buf1.at[d - 1], at.along_x[d - 1])
+        send(acc0.at[:, pl.ds((at.y + d) % 4 * 32, 32), :], buf1.at[d - 1], at.along_y[d - 1])
         for d in (1, 2, 3)
     ]
+    send_rims(pl.ds(1, 2), (0, 1))
+    send_corners(at.near_corners)
     arrive(s1)
-    acc1[...] = acc0[:, pl.ds(at.x * 32, 32), :] + buf1[0] + buf1[1] + buf1[2]
+    acc1[...] = acc0[:, pl.ds(at.y * 32, 32), :] + buf1[0] + buf1[1] + buf1[2]
     s2 = [
-        send(acc1.at[:, pl.ds((at.y + d) % 4 * 8, 8), :], buf2.at[d - 1], at.along_y[d - 1])
+        send(acc1.at[:, pl.ds((at.x + d) % 4 * 8, 8), :], buf2.at[d - 1], at.along_x[d - 1])
         for d in (1, 2, 3)
     ]
     arrive(s2)
-    acc2[...] = acc1[:, pl.ds(at.y * 8, 8), :] + buf2[0] + buf2[1] + buf2[2]
+    acc2[...] = acc1[:, pl.ds(at.x * 8, 8), :] + buf2[0] + buf2[1] + buf2[2]
     buf3[at.z] = acc2[...]
     s3 = [send(acc2, buf3.at[at.z], at.along_z[d - 1]) for d in (1, 2, 3)]
+    send_corners(at.far_corners)
 
     def finish_object():
         arrive(rims)
         for j, (side, near) in enumerate(((before, 2), (after, 3))):
             for half, (level, over, corner) in enumerate(
-                ((above, 0, 4 + j), (below, 1, 6 + j))
+                ((above, 0, j), (below, 1, 2 + j))
             ):
                 rows = pl.ds(HALF * half, HALF)
                 sums = []
@@ -283,7 +307,7 @@
                         grad[ch, 1 + j, pl.ds(HALF + HALF * half, HALF), :]
                         + jnp.where(level, rims_in[over][ch, j], 0.0)
                         + jnp.where(side, rims_in[near][ch, 0, rows, :], 0.0)
-                        + jnp.where(side & level, rims_in[corner][ch, 0], 0.0)
+                        + jnp.where(side & level, corners_in[corner, ch, 0], 0.0)
                     )
                 weight = sums[2] + 1.0
                 for part in range(2):
@@ -294,22 +318,23 @@
                     else:
                         new[part, 1 + j, place, :] = cells
 
+    arrive(s3)
+    total = buf3[0] + buf3[1] + buf3[2] + buf3[3]
+    mine = pl.ds(base_x, 8)
+    probe_new[:, mine, :] = probe[:, mine, :] - total[:2] / (total[2:] + 1.0)
+    part = probe_new.at[:, mine, :]
+    arrive([send(part, part, peer) for peer in at.along_x])
+    part = probe_new.at[:, pl.ds(base_y, 32), :]
+    s5 = [send(part, part, peer) for peer in at.along_y]
     if not last:
         finish_object()
         halo = send_halo(send, at, new)
-    arrive(s3)
-    total = buf3[0] + buf3[1] + buf3[2] + buf3[3]
-    mine = pl.ds(base_y, 8)
-    probe_new[:, mine, :] = probe[:, mine, :] - total[:2] / (total[2:] + 1.0)
-    part = probe_new.at[:, mine, :]
-    arrive([send(part, part, peer) for peer in at.along_y])
-    part = probe_new.at[:, pl.ds(base_x, 32), :]
-    s5 = [send(part, part, peer) for peer in at.along_x]
+    arrive(s5)
+    part = probe_new.at[:, pl.ds(base, 128), :]
+    s6 = send(part, part, at.twin)
     if last:
         finish_object()
-    arrive(s5)
-    part = probe_new.at[:, pl.ds(base, 128), :]
-    arrive([send(part, part, at.twin)])
+    s6.wait_recv()
     if not last:
         arrive(halo)
     send.close()
@@ -337,7 +362,7 @@
 
 def step(last, grad, psum, old, probe):
     shape = (2, F, F) if last else (2, 4, ROWS, 128)
-    copies = 25 if last else 33
+    copies = 27 if last else 35
     return pl.pallas_call(
         functools.partial(step_kernel, last),
         out_shape=(jax.ShapeDtypeStruct(shape, f32), jax.ShapeDtypeStruct((2, F, F), f32)),
@@ -346,7 +371,7 @@
         scratch_shapes=[
             *(pltpu.VMEM((3, 2, HALF, 128), f32) for _ in range(2)),
             *(pltpu.VMEM((3, 1, F, 128), f32) for _ in range(2)),
-            *(pltpu.VMEM((3, 1, HALF, 128), f32) for _ in range(4)),
+            pltpu.VMEM((4, 3, 1, HALF, 128), f32),
             pltpu.VMEM((3, 128, F), f32),
             pltpu.VMEM((3, 128, F), f32),
             pltpu.VMEM((3, 32, F), f32),

time: 169 us -> 162 us (0.959)
  Pallas kernels: 165 us -> 158 us
    pallas_call x2, Pallas kernels: 127 us -> 97.8 us  [step(): pl.pallas_call(functools.partial(step_kernel, last), out_shape=(jax.Shape...]
    pallas_call x2, Pallas kernels: 11.3 us -> 33.4 us  [slots(): pl.pallas_call(slots_kernel, out_shape=(jax.ShapeDtypeStruct((3, 4, ROWS,...]
where the time goes in v4:
time: 162 us
  Pallas kernels  158 us (98%)
  local copies, waits for them, and re-layouts  2.93 us (2%)
    pallas_call x2, Pallas kernels, step(): pl.pallas_call(functools.partial(step_kernel, last), out_shape=(jax.Shape...  97.8 us
    pallas_call x2, Pallas kernels, slots(): pl.pallas_call(slots_kernel, out_shape=(jax.ShapeDtypeStruct((3, 4, ROWS,...  33.4 us
    pallas_call x1, Pallas kernels, open_halo(): pl.pallas_call(open_kernel, out_shape=jax.ShapeDtypeStruct((2, 4, ROWS, 1...  26.6 us

profile of v4, /device:TPU:1, one launch (start us, length us, event | category | flops | bytes accessed | tf_op | source)
XLA Modules:
  0.0 162.3 jit_solution(5692418034039680123)
XLA Ops:
  0.6 0.0 copy-start.2
  0.6 0.0 copy-start.3
  0.7 0.0 copy-start.1
  0.7 0.0 copy-start
  1.5 0.0 copy-start.4
  1.5 1.3 copy-done.4
  2.8 0.0 copy-start.5
  2.8 26.6 %shard_map.86.ext.old = f32[2,4,768,128]{3,2,1,0:T(8,128)S(1)} custom-call(f32[2,256,256]{2,1,0:T(8,128)S(1)} %copy-done.4), custom_call_target="tpu_custom_call" | custom-call | tf_op jit(solution)/shard_map/pallas_call | solution.py:351
  29.4 0.0 copy-done.2
  29.4 0.0 copy-done.3
  29.4 0.0 copy-done.1
  29.4 0.0 copy-done
  29.4 0.0 copy-done.5
  29.4 16.7 %shard_map.87 = (f32[3,4,768,128]{3,2,1,0:T(8,128)S(1)}, f32[3,256,256]{2,1,0:T(8,128)S(1)}) custom-call(s32[2,16]{1,0:T(2,128)S(1)} %bitcast.9, s32[1]{0:T(128)} %bitcast.5.load, bf16[16,256,256]{2,1,0:T(8,128)(2,1)S(1)} %bitcast.7, f32[2,4,768,128]{3,2,1,0:T(8,128)S(1)} %shard_map.86.ext.old, f32[2,256,256]{2,1,0:T(8,128)S(1)} %copy-done.1, ...), custom_call_target="tpu_custom_call" | custom-call | tf_op jit(solution)/shard_map/pallas_call | solution.py:107
  46.1 55.3 %shard_map.88 = (f32[2,4,768,128]{3,2,1,0:T(8,128)S(1)}, f32[2,256,256]{2,1,0:T(8,128)S(1)}) custom-call(f32[3,4,768,128]{3,2,1,0:T(8,128)S(1)} %get-tuple-element.8.grad, f32[3,256,256]{2,1,0:T(8,128)S(1)} %get-tuple-element.9.psum, f32[2,4,768,128]{3,2,1,0:T(8,128)S(1)} %shard_map.86.ext.old, f32[2,256,256]{2,1,0:T(8,128)S(1)} %copy-done.1), custom_call_target="tpu_custom_call" | custom-call | tf_op jit(solution)/shard_map/pallas_call | solution.py:366
  101.5 16.7 %shard_map.89 = (f32[3,4,768,128]{3,2,1,0:T(8,128)S(1)}, f32[3,256,256]{2,1,0:T(8,128)S(1)}) custom-call(s32[2,16]{1,0:T(2,128)S(1)} %bitcast.10, s32[1]{0:T(128)} %bitcast.6.load, bf16[16,256,256]{2,1,0:T(8,128)(2,1)S(1)} %bitcast.8, f32[2,4,768,128]{3,2,1,0:T(8,128)S(1)} %get-tuple-element.10.ext.old, f32[2,256,256]{2,1,0:T(8,128)S(1)} %get-tuple-element.11.probe, ...), custom_call_target="tpu_custom_call" | custom-call | tf_op jit(solution)/shard_map/pallas_call | solution.py:107
  118.2 42.5 %shard_map.90 = (f32[2,256,256]{2,1,0:T(8,128)S(1)}, f32[2,256,256]{2,1,0:T(8,128)S(1)}) custom-call(f32[3,4,768,128]{3,2,1,0:T(8,128)S(1)} %get-tuple-element.12.grad, f32[3,256,256]{2,1,0:T(8,128)S(1)} %get-tuple-element.13.psum, f32[2,4,768,128]{3,2,1,0:T(8,128)S(1)} %get-tuple-element.10.ext.old, f32[2,256,256]{2,1,0:T(8,128)S(1)} %get-tuple-element.11.probe), custom_call_target="tpu_custom_call" | custom-call | tf_op jit(solution)/shard_map/pallas_call | solution.py:366
  160.7 0.8 copy.12
  161.5 0.8 copy.13
Async XLA Ops:
  0.6 28.8 %copy-start.2 = (bf16[512,512]{1,0:T(8,128)(2,1)S(1)}, bf16[512,512]{1,0:T(8,128)(2,1)}, u32[]{:S(2)}) copy-start(bf16[512,512]{1,0:T(8,128)(2,1)} %constant.5.clone.inv) | copy-start | bytes 1572868
  0.6 28.8 %copy-start.3 = (bf16[512,512]{1,0:T(8,128)(2,1)S(1)}, bf16[512,512]{1,0:T(8,128)(2,1)}, u32[]{:S(2)}) copy-start(bf16[512,512]{1,0:T(8,128)(2,1)} %constant.4.clone.fwd) | copy-start | bytes 1572868
  0.7 28.8 %copy-start.1 = (f32[2,256,256]{2,1,0:T(8,128)S(1)}, f32[2,256,256]{2,1,0:T(8,128)}, u32[]{:S(2)}) copy-start(f32[2,256,256]{2,1,0:T(8,128)} %probe.3) | copy-start | bytes 1572868
  0.7 28.8 %copy-start = (bf16[1,1,16,256,256]{4,3,2,1,0:T(8,128)(2,1)S(1)}, bf16[1,1,16,256,256]{4,3,2,1,0:T(8,128)(2,1)}, u32[]{:S(2)}) copy-start(bf16[1,1,16,256,256]{4,3,2,1,0:T(8,128)(2,1)} %param.9) | copy-start | bytes 6291460
  1.5 1.3 copy-start.4
  2.8 26.6 %copy-start.5 = (s32[1,1,16,2]{2,3,1,0:T(2,128)S(1)}, s32[1,1,16,2]{2,3,1,0:T(2,128)}, u32[]{:S(2)}) copy-start(s32[1,1,16,2]{2,3,1,0:T(2,128)} %param.7) | copy-start | bytes 388

commit v5 on v3

--- a/solution.py
+++ b/solution.py
@@ -118,6 +118,10 @@
 TILE = slice(HALF, HALF + F)
 
 
+TOP, BOTTOM = pl.ds(HALF, HALF), pl.ds(F, HALF)
+ABOVE, BELOW = pl.ds(0, HALF), pl.ds(F + HALF, HALF)
+
+
 class Places:
     def __init__(self):
         row, col = lax.axis_index("row"), lax.axis_index("col")
@@ -127,14 +131,16 @@
         self.x, z_hi, self.core = col // 4, col // 2 % 2, col % 2
         self.z = z_hi * 2 + z_lo
         self.up, self.down = ((row + n_row - 1) % n_row, col), ((row + 1) % n_row, col)
-        self.left, self.right = (row, (col + n_col - 1) % n_col), (row, (col + 1) % n_col)
-        north, south = self.up[0], self.down[0]
-        west, east = self.left[1], self.right[1]
+        self.twin = (row, col + 1 - 2 * self.core)
+        self.far = (row, (col + n_col - 1 + 2 * self.core) % n_col)
+        self.near_north, self.near_south = (self.up[0], self.twin[1]), (self.down[0], self.twin[1])
+        self.far_north, self.far_south = (self.up[0], self.far[1]), (self.down[0], self.far[1])
         self.around = (
-            self.up, self.down, self.left, self.right,
-            (north, west), (north, east), (south, west), (south, east),
+            self.up, self.down, self.twin, self.far,
+            self.near_north, self.near_south, self.far_north, self.far_south,
         )
-        self.twin = (row, col + 1 - 2 * self.core)
+        self.near_rim, self.far_rim = 3 - 3 * self.core, 3 * self.core
+        self.near_edge, self.far_edge = 2 - self.core, 1 + self.core
         self.along_x = [(row, (self.x + d) % 4 * 4 + col % 4) for d in (1, 2, 3)]
         self.along_y = [(z_lo * 4 + (self.y + d) % 4, col) for d in (1, 2, 3)]
         self.along_z = []
@@ -179,29 +185,23 @@
         copy.wait_recv()
 
 
-TOP, BOTTOM = pl.ds(HALF, HALF), pl.ds(F, HALF)
-ABOVE, BELOW = pl.ds(0, HALF), pl.ds(F + HALF, HALF)
 INNER = pl.ds(HALF, F)
-WEST, EAST = pl.ds(0, 1), pl.ds(3, 1)
-FIRST, SECOND, BOTH = pl.ds(1, 1), pl.ds(2, 1), pl.ds(1, 2)
-OUTSIDE = (
-    (BOTH, ABOVE), (BOTH, BELOW), (WEST, INNER), (EAST, INNER),
-    (WEST, ABOVE), (EAST, ABOVE), (WEST, BELOW), (EAST, BELOW),
-)
-INSIDE = (
-    (BOTH, TOP), (BOTH, BOTTOM), (FIRST, INNER), (SECOND, INNER),
-    (FIRST, TOP), (SECOND, TOP), (FIRST, BOTTOM), (SECOND, BOTTOM),
-)
-OPPOSITE = (1, 0, 3, 2, 7, 6, 5, 4)
+BOTH = pl.ds(1, 2)
 
 
 def send_halo(send, at, ext):
-    copies = []
-    for k, peer in enumerate(at.around):
-        tiles, rows = INSIDE[k]
-        there, below = OUTSIDE[OPPOSITE[k]]
-        copies.append(send(ext.at[:, tiles, rows, :], ext.at[:, there, below, :], peer))
-    return copies
+    near, far = pl.ds(at.near_edge, 1), pl.ds(at.far_edge, 1)
+    there_near, there_far = pl.ds(at.far_rim, 1), pl.ds(at.near_rim, 1)
+    return [
+        send(ext.at[:, far, INNER, :], ext.at[:, there_far, INNER, :], at.far),
+        send(ext.at[:, BOTH, TOP, :], ext.at[:, BOTH, BELOW, :], at.up),
+        send(ext.at[:, BOTH, BOTTOM, :], ext.at[:, BOTH, ABOVE, :], at.down),
+        send(ext.at[:, far, TOP, :], ext.at[:, there_far, BELOW, :], at.far_north),
+        send(ext.at[:, far, BOTTOM, :], ext.at[:, there_far, ABOVE, :], at.far_south),
+        send(ext.at[:, near, INNER, :], ext.at[:, there_near, INNER, :], at.twin),
+        send(ext.at[:, near, TOP, :], ext.at[:, there_near, BELOW, :], at.near_north),
+        send(ext.at[:, near, BOTTOM, :], ext.at[:, there_near, ABOVE, :], at.near_south),
+    ]
 
 
 def clear_outside(at, ext):
@@ -237,79 +237,103 @@
 
 
 def step_kernel(last, grad, psum, old, probe, new, probe_new, *scratch):
-    rims_in, (acc0, buf0, acc1, buf1, acc2, buf2, buf3, send_sem, recv_sem) = scratch[:8], scratch[8:]
+    from_up, from_down, sides_in, far_in, side, strips = scratch[:6]
+    acc0, buf0, acc1, buf1, acc2, buf2, buf3, send_sem, recv_sem = scratch[6:]
     at = Places()
-    meet((*at.around, at.twin, *at.along_x, *at.along_y, *at.along_z))
+    meet((*at.around, *at.along_x, *at.along_y, *at.along_z))
     send = Sender(send_sem, recv_sem)
     above, below = at.row > 0, at.row < at.n_row - 1
     before, after = at.col > 0, at.col < at.n_col - 1
     base = at.core * 128
     base_x = base + at.x * 32
     base_y = base_x + at.y * 8
+    near_rim, far_rim = pl.ds(at.near_rim, 1), pl.ds(at.far_rim, 1)
+    far_edge = pl.ds(at.far_edge, 1)
+    near_part, far_part = pl.ds(at.near_edge - 1, 1), pl.ds(at.far_edge - 1, 1)
 
     s0 = send(psum.at[:, pl.ds(128 - base, 128), :], buf0, at.twin)
-    rims = []
-    for k, peer in enumerate(at.around):
-        tiles, rows = OUTSIDE[k]
-        rims.append(send(grad.at[:, tiles, rows, :], rims_in[OPPOSITE[k]], peer))
-
+    twins = send(grad.at[:, near_rim, : 2 * F, :], sides_in.at[at.core], at.twin)
+    corners = [
+        send(grad.at[:, far_rim, ABOVE, :], far_in.at[1], at.up),
+        send(grad.at[:, far_rim, BELOW, :], far_in.at[0], at.down),
+    ]
+    rims = [
+        send(grad.at[:, far_edge, ABOVE, :], from_down.at[:, far_part], at.up),
+        send(grad.at[:, far_edge, BELOW, :], from_up.at[:, far_part], at.down),
+    ]
     s0.wait_recv()
     acc0[...] = psum[:, pl.ds(base, 128), :] + buf0[...]
     s1 = [
         send(acc0.at[:, pl.ds((at.x + d) % 4 * 32, 32), :], buf1.at[d - 1], at.along_x[d - 1])
         for d in (1, 2, 3)
     ]
+    twins.wait_recv()
+    for ch in range(3):
+        for k, rows in enumerate((ABOVE, BELOW)):
+            strips[k, ch, 0] = grad[ch, at.near_edge, rows, :] + sides_in[1 - at.core, ch, 0, rows, :]
+
+    def send_side():
+        rims.append(send(side, sides_in.at[1 - at.core, :, :, INNER, :], at.far))
+
+    arrive(corners)
+    for ch in range(3):
+        side[ch, 0, :HALF, :] = grad[ch, at.far_rim, TOP, :] + jnp.where(above, far_in[0, ch, 0], 0.0)
+        side[ch, 0, HALF:, :] = grad[ch, at.far_rim, BOTTOM, :] + jnp.where(below, far_in[1, ch, 0], 0.0)
+    if not last:
+        send_side()
     arrive(s1)
     acc1[...] = acc0[:, pl.ds(at.x * 32, 32), :] + buf1[0] + buf1[1] + buf1[2]
     s2 = [
         send(acc1.at[:, pl.ds((at.y + d) % 4 * 8, 8), :], buf2.at[d - 1], at.along_y[d - 1])
         for d in (1, 2, 3)
     ]
+    rims.append(send(strips.at[0], from_down.at[:, near_part], at.up))
+    rims.append(send(strips.at[1], from_up.at[:, near_part], at.down))
     arrive(s2)
     acc2[...] = acc1[:, pl.ds(at.y * 8, 8), :] + buf2[0] + buf2[1] + buf2[2]
     buf3[at.z] = acc2[...]
     s3 = [send(acc2, buf3.at[at.z], at.along_z[d - 1]) for d in (1, 2, 3)]
+    if last:
+        send_side()
 
     def finish_object():
         arrive(rims)
-        for j, (side, near) in enumerate(((before, 2), (after, 3))):
-            for half, (level, over, corner) in enumerate(
-                ((above, 0, 4 + j), (below, 1, 6 + j))
-            ):
+        for j, beside in enumerate((before, after)):
+            for half, (level, rim) in enumerate(((above, from_up), (below, from_down))):
                 rows = pl.ds(HALF * half, HALF)
+                place = pl.ds(HALF + HALF * half, HALF)
                 sums = []
                 for ch in range(3):
                     sums.append(
-                        grad[ch, 1 + j, pl.ds(HALF + HALF * half, HALF), :]
-                        + jnp.where(level, rims_in[over][ch, j], 0.0)
-                        + jnp.where(side, rims_in[near][ch, 0, rows, :], 0.0)
-                        + jnp.where(side & level, rims_in[corner][ch, 0], 0.0)
+                        grad[ch, 1 + j, place, :]
+                        + jnp.where(level, rim[ch, j], 0.0)
+                        + jnp.where(beside, sides_in[j, ch, 0, place, :], 0.0)
                     )
                 weight = sums[2] + 1.0
                 for part in range(2):
-                    place = pl.ds(HALF + HALF * half, HALF)
                     cells = old[part, 1 + j, place, :] - sums[part] / weight
                     if last:
                         new[part, rows, 128 * j : 128 * j + 128] = cells
                     else:
                         new[part, 1 + j, place, :] = cells
 
-    if not last:
-        finish_object()
-        halo = send_halo(send, at, new)
     arrive(s3)
     total = buf3[0] + buf3[1] + buf3[2] + buf3[3]
     mine = pl.ds(base_y, 8)
     probe_new[:, mine, :] = probe[:, mine, :] - total[:2] / (total[2:] + 1.0)
     part = probe_new.at[:, mine, :]
-    arrive([send(part, part, peer) for peer in at.along_y])
+    s4 = [send(part, part, peer) for peer in at.along_y]
+    if not last:
+        finish_object()
+        halo = send_halo(send, at, new)
+    arrive(s4)
     part = probe_new.at[:, pl.ds(base_x, 32), :]
-    s5 = [send(part, part, peer) for peer in at.along_x]
+    arrive([send(part, part, peer) for peer in at.along_x])
+    part = probe_new.at[:, pl.ds(base, 128), :]
+    s6 = send(part, part, at.twin)
     if last:
         finish_object()
-    arrive(s5)
-    part = probe_new.at[:, pl.ds(base, 128), :]
-    arrive([send(part, part, at.twin)])
+    s6.wait_recv()
     if not last:
         arrive(halo)
     send.close()
@@ -344,9 +368,12 @@
         in_specs=[VMEM] * 4,
         out_specs=(VMEM, VMEM),
         scratch_shapes=[
-            *(pltpu.VMEM((3, 2, HALF, 128), f32) for _ in range(2)),
-            *(pltpu.VMEM((3, 1, F, 128), f32) for _ in range(2)),
-            *(pltpu.VMEM((3, 1, HALF, 128), f32) for _ in range(4)),
+            pltpu.VMEM((3, 2, HALF, 128), f32),
+            pltpu.VMEM((3, 2, HALF, 128), f32),
+            pltpu.VMEM((2, 3, 1, 2 * F, 128), f32),
+            pltpu.VMEM((2, 3, 1, HALF, 128), f32),
+            pltpu.VMEM((3, 1, F, 128), f32),
+            pltpu.VMEM((2, 3, 1, HALF, 128), f32),
             pltpu.VMEM((3, 128, F), f32),
             pltpu.VMEM((3, 128, F), f32),
             pltpu.VMEM((3, 32, F), f32),

time: 169 us -> 148 us (0.88)
  Pallas kernels: 165 us -> 143 us
    pallas_call x2, Pallas kernels: 127 us -> 90.2 us  [step(): pl.pallas_call(functools.partial(step_kernel, last), out_shape=(jax.Shape...]
    pallas_call x2, Pallas kernels: 11.3 us -> 26.3 us  [slots(): pl.pallas_call(slots_kernel, out_shape=(jax.ShapeDtypeStruct((3, 4, ROWS,...]
where the time goes in v5:
time: 148 us
  Pallas kernels  143 us (97%)
  local copies, waits for them, and re-layouts  2.93 us (2%)
  between operations  1.55 us (1%)
    pallas_call x2, Pallas kernels, step(): pl.pallas_call(functools.partial(step_kernel, last), out_shape=(jax.Shape...  90.2 us
    pallas_call x1, Pallas kernels, open_halo(): pl.pallas_call(open_kernel, out_shape=jax.ShapeDtypeStruct((2, 4, ROWS, 1...  26.6 us
    pallas_call x2, Pallas kernels, slots(): pl.pallas_call(slots_kernel, out_shape=(jax.ShapeDtypeStruct((3, 4, ROWS,...  26.3 us

profile of v5, /device:TPU:1, one launch (start us, length us, event | category | flops | bytes accessed | tf_op | source)
XLA Modules:
  0.0 147.6 jit_solution(10654733600761892554)
XLA Ops:
  0.6 0.0 copy-start.2
  0.6 0.0 copy-start.3
  0.7 0.0 copy-start.1
  0.7 0.0 copy-start
  1.5 0.0 copy-start.4
  1.5 1.3 copy-done.4
  2.8 0.0 copy-start.5
  2.8 26.6 %shard_map.86.ext.old = f32[2,4,768,128]{3,2,1,0:T(8,128)S(1)} custom-call(f32[2,256,256]{2,1,0:T(8,128)S(1)} %copy-done.4), custom_call_target="tpu_custom_call" | custom-call | tf_op jit(solution)/shard_map/pallas_call | solution.py:350
  29.4 0.0 copy-done.2
  29.4 0.0 copy-done.3
  29.4 0.0 copy-done.1
  29.4 0.0 copy-done
  29.4 0.0 copy-done.5
  29.5 13.2 %shard_map.87 = (f32[3,4,768,128]{3,2,1,0:T(8,128)S(1)}, f32[3,256,256]{2,1,0:T(8,128)S(1)}) custom-call(s32[2,16]{1,0:T(2,128)S(1)} %bitcast.9, s32[1]{0:T(128)} %bitcast.5.load, bf16[16,256,256]{2,1,0:T(8,128)(2,1)S(1)} %bitcast.7, f32[2,4,768,128]{3,2,1,0:T(8,128)S(1)} %shard_map.86.ext.old, f32[2,256,256]{2,1,0:T(8,128)S(1)} %copy-done.1, ...), custom_call_target="tpu_custom_call" | custom-call | tf_op jit(solution)/shard_map/pallas_call | solution.py:107
  42.6 51.6 %shard_map.88 = (f32[2,4,768,128]{3,2,1,0:T(8,128)S(1)}, f32[2,256,256]{2,1,0:T(8,128)S(1)}) custom-call(f32[3,4,768,128]{3,2,1,0:T(8,128)S(1)} %get-tuple-element.8.grad, f32[3,256,256]{2,1,0:T(8,128)S(1)} %get-tuple-element.9.psum, f32[2,4,768,128]{3,2,1,0:T(8,128)S(1)} %shard_map.86.ext.old, f32[2,256,256]{2,1,0:T(8,128)S(1)} %copy-done.1), custom_call_target="tpu_custom_call" | custom-call | tf_op jit(solution)/shard_map/pallas_call | solution.py:365
  94.3 13.2 %shard_map.89 = (f32[3,4,768,128]{3,2,1,0:T(8,128)S(1)}, f32[3,256,256]{2,1,0:T(8,128)S(1)}) custom-call(s32[2,16]{1,0:T(2,128)S(1)} %bitcast.10, s32[1]{0:T(128)} %bitcast.6.load, bf16[16,256,256]{2,1,0:T(8,128)(2,1)S(1)} %bitcast.8, f32[2,4,768,128]{3,2,1,0:T(8,128)S(1)} %get-tuple-element.10.ext.old, f32[2,256,256]{2,1,0:T(8,128)S(1)} %get-tuple-element.11.probe, ...), custom_call_target="tpu_custom_call" | custom-call | tf_op jit(solution)/shard_map/pallas_call | solution.py:107
  107.4 38.5 %shard_map.90 = (f32[2,256,256]{2,1,0:T(8,128)S(1)}, f32[2,256,256]{2,1,0:T(8,128)S(1)}) custom-call(f32[3,4,768,128]{3,2,1,0:T(8,128)S(1)} %get-tuple-element.12.grad, f32[3,256,256]{2,1,0:T(8,128)S(1)} %get-tuple-element.13.psum, f32[2,4,768,128]{3,2,1,0:T(8,128)S(1)} %get-tuple-element.10.ext.old, f32[2,256,256]{2,1,0:T(8,128)S(1)} %get-tuple-element.11.probe), custom_call_target="tpu_custom_call" | custom-call | tf_op jit(solution)/shard_map/pallas_call | solution.py:365
  146.0 0.8 copy.12
  146.8 0.8 copy.13
Async XLA Ops:
  0.6 28.8 %copy-start.2 = (bf16[512,512]{1,0:T(8,128)(2,1)S(1)}, bf16[512,512]{1,0:T(8,128)(2,1)}, u32[]{:S(2)}) copy-start(bf16[512,512]{1,0:T(8,128)(2,1)} %constant.5.clone.inv) | copy-start | bytes 1572868
  0.6 28.8 %copy-start.3 = (bf16[512,512]{1,0:T(8,128)(2,1)S(1)}, bf16[512,512]{1,0:T(8,128)(2,1)}, u32[]{:S(2)}) copy-start(bf16[512,512]{1,0:T(8,128)(2,1)} %constant.4.clone.fwd) | copy-start | bytes 1572868
  0.7 28.8 %copy-start.1 = (f32[2,256,256]{2,1,0:T(8,128)S(1)}, f32[2,256,256]{2,1,0:T(8,128)}, u32[]{:S(2)}) copy-start(f32[2,256,256]{2,1,0:T(8,128)} %probe.3) | copy-start | bytes 1572868
  0.7 28.8 %copy-start = (bf16[1,1,16,256,256]{4,3,2,1,0:T(8,128)(2,1)S(1)}, bf16[1,1,16,256,256]{4,3,2,1,0:T(8,128)(2,1)}, u32[]{:S(2)}) copy-start(bf16[1,1,16,256,256]{4,3,2,1,0:T(8,128)(2,1)} %param.9) | copy-start | bytes 6291460
  1.5 1.3 copy-start.4
  2.8 26.7 %copy-start.5 = (s32[1,1,16,2]{2,3,1,0:T(2,128)S(1)}, s32[1,1,16,2]{2,3,1,0:T(2,128)}, u32[]{:S(2)}) copy-start(s32[1,1,16,2]{2,3,1,0:T(2,128)} %param.7) | copy-start | bytes 388

commit v6 on v5

--- a/solution.py
+++ b/solution.py
@@ -139,6 +139,12 @@
             self.up, self.down, self.twin, self.far,
             self.near_north, self.near_south, self.far_north, self.far_south,
         )
+        self.above, self.below = row > 0, row < n_row - 1
+        self.aside = (col > 0) & (col < n_col - 1)
+        self.over, self.under = row == n_row // 2, row == n_row // 2 - 1
+        self.first, self.final = row == 0, row == n_row - 1
+        self.row_first, self.row_final = (0 * row, col), (0 * row + n_row - 1, col)
+        self.row_under, self.row_over = (0 * row + n_row // 2 - 1, col), (0 * row + n_row // 2, col)
         self.near_rim, self.far_rim = 3 - 3 * self.core, 3 * self.core
         self.near_edge, self.far_edge = 2 - self.core, 1 + self.core
         self.along_x = [(row, (self.x + d) % 4 * 4 + col % 4) for d in (1, 2, 3)]
@@ -156,12 +162,19 @@
     pl.semaphore_wait(barrier, len(peers))
 
 
+def run_if(condition, action):
+    if condition is None:
+        action()
+    else:
+        pl.when(condition)(action)
+
+
 class Sender:
     def __init__(self, send_sem, recv_sem):
         self.send_sem, self.recv_sem, self.used = send_sem, recv_sem, 0
         self.open = []
 
-    def __call__(self, src, dst, peer):
+    def __call__(self, src, dst, peer, sends=None, gets=None):
         copy = pltpu.make_async_remote_copy(
             src_ref=src,
             dst_ref=dst,
@@ -171,18 +184,18 @@
             device_id_type=MESH,
         )
         self.used += 1
-        copy.start()
-        self.open.append(copy)
-        return copy
+        run_if(sends, copy.start)
+        self.open.append((copy, sends))
+        return copy, gets
 
     def close(self):
-        for copy in self.open:
-            copy.wait_send()
+        for copy, sends in self.open:
+            run_if(sends, copy.wait_send)
 
 
 def arrive(copies):
-    for copy in copies:
-        copy.wait_recv()
+    for copy, gets in copies:
+        run_if(gets, copy.wait_recv)
 
 
 INNER = pl.ds(HALF, F)
@@ -192,15 +205,17 @@
 def send_halo(send, at, ext):
     near, far = pl.ds(at.near_edge, 1), pl.ds(at.far_edge, 1)
     there_near, there_far = pl.ds(at.far_rim, 1), pl.ds(at.near_rim, 1)
+    up, down, aside = (at.above, at.below), (at.below, at.above), (at.aside, at.aside)
+    up_aside, down_aside = (at.above & at.aside, at.below & at.aside), (at.below & at.aside, at.above & at.aside)
     return [
-        send(ext.at[:, far, INNER, :], ext.at[:, there_far, INNER, :], at.far),
-        send(ext.at[:, BOTH, TOP, :], ext.at[:, BOTH, BELOW, :], at.up),
-        send(ext.at[:, BOTH, BOTTOM, :], ext.at[:, BOTH, ABOVE, :], at.down),
-        send(ext.at[:, far, TOP, :], ext.at[:, there_far, BELOW, :], at.far_north),
-        send(ext.at[:, far, BOTTOM, :], ext.at[:, there_far, ABOVE, :], at.far_south),
+        send(ext.at[:, far, INNER, :], ext.at[:, there_far, INNER, :], at.far, *aside),
+        send(ext.at[:, BOTH, TOP, :], ext.at[:, BOTH, BELOW, :], at.up, *up),
+        send(ext.at[:, BOTH, BOTTOM, :], ext.at[:, BOTH, ABOVE, :], at.down, *down),
+        send(ext.at[:, far, TOP, :], ext.at[:, there_far, BELOW, :], at.far_north, *up_aside),
+        send(ext.at[:, far, BOTTOM, :], ext.at[:, there_far, ABOVE, :], at.far_south, *down_aside),
         send(ext.at[:, near, INNER, :], ext.at[:, there_near, INNER, :], at.twin),
-        send(ext.at[:, near, TOP, :], ext.at[:, there_near, BELOW, :], at.near_north),
-        send(ext.at[:, near, BOTTOM, :], ext.at[:, there_near, ABOVE, :], at.near_south),
+        send(ext.at[:, near, TOP, :], ext.at[:, there_near, BELOW, :], at.near_north, *up),
+        send(ext.at[:, near, BOTTOM, :], ext.at[:, there_near, ABOVE, :], at.near_south, *down),
     ]
 
 
@@ -237,12 +252,13 @@
 
 
 def step_kernel(last, grad, psum, old, probe, new, probe_new, *scratch):
-    from_up, from_down, sides_in, far_in, side, strips = scratch[:6]
-    acc0, buf0, acc1, buf1, acc2, buf2, buf3, send_sem, recv_sem = scratch[6:]
+    from_up, from_down, sides_in, far_in, side, strips, relay = scratch[:7]
+    acc0, buf0, acc1, buf1, acc2, buf2, buf3, send_sem, recv_sem = scratch[7:]
     at = Places()
     meet((*at.around, *at.along_x, *at.along_y, *at.along_z))
     send = Sender(send_sem, recv_sem)
-    above, below = at.row > 0, at.row < at.n_row - 1
+    above, below = at.above, at.below
+    up, down = (above, below), (below, above)
     before, after = at.col > 0, at.col < at.n_col - 1
     base = at.core * 128
     base_x = base + at.x * 32
@@ -254,47 +270,64 @@
     s0 = send(psum.at[:, pl.ds(128 - base, 128), :], buf0, at.twin)
     twins = send(grad.at[:, near_rim, : 2 * F, :], sides_in.at[at.core], at.twin)
     corners = [
-        send(grad.at[:, far_rim, ABOVE, :], far_in.at[1], at.up),
-        send(grad.at[:, far_rim, BELOW, :], far_in.at[0], at.down),
+        send(grad.at[:, far_rim, ABOVE, :], far_in.at[1], at.up, *up),
+        send(grad.at[:, far_rim, BELOW, :], far_in.at[0], at.down, *down),
     ]
     rims = [
-        send(grad.at[:, far_edge, ABOVE, :], from_down.at[:, far_part], at.up),
-        send(grad.at[:, far_edge, BELOW, :], from_up.at[:, far_part], at.down),
-    ]
-    s0.wait_recv()
+        send(grad.at[:, far_edge, ABOVE, :], from_down.at[:, far_part], at.up, *up),
+        send(grad.at[:, far_edge, BELOW, :], from_up.at[:, far_part], at.down, *down),
+    ]
+    arrive([s0])
     acc0[...] = psum[:, pl.ds(base, 128), :] + buf0[...]
     s1 = [
         send(acc0.at[:, pl.ds((at.x + d) % 4 * 32, 32), :], buf1.at[d - 1], at.along_x[d - 1])
         for d in (1, 2, 3)
     ]
-    twins.wait_recv()
+    arrive([twins])
     for ch in range(3):
         for k, rows in enumerate((ABOVE, BELOW)):
             strips[k, ch, 0] = grad[ch, at.near_edge, rows, :] + sides_in[1 - at.core, ch, 0, rows, :]
 
+    relays = [
+        send(strips.at[0], relay, at.row_first, at.over, at.first),
+        send(strips.at[1], relay, at.row_final, at.under, at.final),
+    ]
+
+    def send_near():
+        rims.extend([
+            send(strips.at[0], from_down.at[:, near_part], at.up, above & ~at.over, below & ~at.under),
+            send(strips.at[1], from_up.at[:, near_part], at.down, below & ~at.under, above & ~at.over),
+        ])
+
+    if not last:
+        send_near()
+
     def send_side():
-        rims.append(send(side, sides_in.at[1 - at.core, :, :, INNER, :], at.far))
+        rims.append(send(side, sides_in.at[1 - at.core, :, :, INNER, :], at.far, at.aside, at.aside))
 
     arrive(corners)
     for ch in range(3):
         side[ch, 0, :HALF, :] = grad[ch, at.far_rim, TOP, :] + jnp.where(above, far_in[0, ch, 0], 0.0)
         side[ch, 0, HALF:, :] = grad[ch, at.far_rim, BOTTOM, :] + jnp.where(below, far_in[1, ch, 0], 0.0)
-    if not last:
-        send_side()
+    send_side()
     arrive(s1)
     acc1[...] = acc0[:, pl.ds(at.x * 32, 32), :] + buf1[0] + buf1[1] + buf1[2]
     s2 = [
         send(acc1.at[:, pl.ds((at.y + d) % 4 * 8, 8), :], buf2.at[d - 1], at.along_y[d - 1])
         for d in (1, 2, 3)
     ]
-    rims.append(send(strips.at[0], from_down.at[:, near_part], at.up))
-    rims.append(send(strips.at[1], from_up.at[:, near_part], at.down))
+    if last:
+        send_near()
     arrive(s2)
     acc2[...] = acc1[:, pl.ds(at.y * 8, 8), :] + buf2[0] + buf2[1] + buf2[2]
     buf3[at.z] = acc2[...]
     s3 = [send(acc2, buf3.at[at.z], at.along_z[d - 1]) for d in (1, 2, 3)]
-    if last:
-        send_side()
+
+    arrive(relays)
+    rims += [
+        send(relay, from_down.at[:, near_part], at.row_under, at.first, at.under),
+        send(relay, from_up.at[:, near_part], at.row_over, at.final, at.over),
+    ]
 
     def finish_object():
         arrive(rims)
@@ -333,7 +366,7 @@
     s6 = send(part, part, at.twin)
     if last:
         finish_object()
-    s6.wait_recv()
+    arrive([s6])
     if not last:
         arrive(halo)
     send.close()
@@ -361,7 +394,7 @@
 
 def step(last, grad, psum, old, probe):
     shape = (2, F, F) if last else (2, 4, ROWS, 128)
-    copies = 25 if last else 33
+    copies = 29 if last else 37
     return pl.pallas_call(
         functools.partial(step_kernel, last),
         out_shape=(jax.ShapeDtypeStruct(shape, f32), jax.ShapeDtypeStruct((2, F, F), f32)),
@@ -374,6 +407,7 @@
             pltpu.VMEM((2, 3, 1, HALF, 128), f32),
             pltpu.VMEM((3, 1, F, 128), f32),
             pltpu.VMEM((2, 3, 1, HALF, 128), f32),
+            pltpu.VMEM((3, 1, HALF, 128), f32),
             pltpu.VMEM((3, 128, F), f32),
             pltpu.VMEM((3, 128, F), f32),
             pltpu.VMEM((3, 32, F), f32),

time: 148 us -> 140 us (0.946)
  Pallas kernels: 143 us -> 136 us
    pallas_call x2, Pallas kernels: 90.2 us -> 77.2 us  [step(): pl.pallas_call(functools.partial(step_kernel, last), out_shape=(jax.Shape...]
    pallas_call x2, Pallas kernels: 26.3 us -> 33.2 us  [slots(): pl.pallas_call(slots_kernel, out_shape=(jax.ShapeDtypeStruct((3, 4, ROWS,...]
where the time goes in v6:
time: 140 us
  Pallas kernels  136 us (97%)
  local copies, waits for them, and re-layouts  2.93 us (2%)
  between operations  1.55 us (1%)
    pallas_call x2, Pallas kernels, step(): pl.pallas_call(functools.partial(step_kernel, last), out_shape=(jax.Shape...  77.2 us
    pallas_call x2, Pallas kernels, slots(): pl.pallas_call(slots_kernel, out_shape=(jax.ShapeDtypeStruct((3, 4, ROWS,...  33.2 us
    pallas_call x1, Pallas kernels, open_halo(): pl.pallas_call(open_kernel, out_shape=jax.ShapeDtypeStruct((2, 4, ROWS, 1...  25.3 us
    unnamed x14, local copies, waits for them, and re-layouts  2.93 us

profile of v6, /device:TPU:1, one launch (start us, length us, event | category | flops | bytes accessed | tf_op | source)
XLA Modules:
  0.0 140.2 jit_solution(15413171802885125888)
XLA Ops:
  0.6 0.0 copy-start.2
  0.6 0.0 copy-start.3
  0.7 0.0 copy-start.1
  0.7 0.0 copy-start
  1.5 0.0 copy-start.4
  1.5 1.3 copy-done.4
  2.8 0.0 copy-start.5
  2.8 25.3 %shard_map.86.ext.old = f32[2,4,768,128]{3,2,1,0:T(8,128)S(1)} custom-call(f32[2,256,256]{2,1,0:T(8,128)S(1)} %copy-done.4), custom_call_target="tpu_custom_call" | custom-call | tf_op jit(solution)/shard_map/pallas_call | solution.py:383
  28.1 0.0 copy-done.2
  28.1 0.0 copy-done.3
  28.1 0.0 copy-done.1
  28.1 0.0 copy-done
  28.1 0.0 copy-done.5
  28.1 16.6 %shard_map.87 = (f32[3,4,768,128]{3,2,1,0:T(8,128)S(1)}, f32[3,256,256]{2,1,0:T(8,128)S(1)}) custom-call(s32[2,16]{1,0:T(2,128)S(1)} %bitcast.9, s32[1]{0:T(128)} %bitcast.5.load, bf16[16,256,256]{2,1,0:T(8,128)(2,1)S(1)} %bitcast.7, f32[2,4,768,128]{3,2,1,0:T(8,128)S(1)} %shard_map.86.ext.old, f32[2,256,256]{2,1,0:T(8,128)S(1)} %copy-done.1, ...), custom_call_target="tpu_custom_call" | custom-call | tf_op jit(solution)/shard_map/pallas_call | solution.py:107
  44.7 40.5 %shard_map.88 = (f32[2,4,768,128]{3,2,1,0:T(8,128)S(1)}, f32[2,256,256]{2,1,0:T(8,128)S(1)}) custom-call(f32[3,4,768,128]{3,2,1,0:T(8,128)S(1)} %get-tuple-element.8.grad, f32[3,256,256]{2,1,0:T(8,128)S(1)} %get-tuple-element.9.psum, f32[2,4,768,128]{3,2,1,0:T(8,128)S(1)} %shard_map.86.ext.old, f32[2,256,256]{2,1,0:T(8,128)S(1)} %copy-done.1), custom_call_target="tpu_custom_call" | custom-call | tf_op jit(solution)/shard_map/pallas_call | solution.py:398
  85.3 16.6 %shard_map.89 = (f32[3,4,768,128]{3,2,1,0:T(8,128)S(1)}, f32[3,256,256]{2,1,0:T(8,128)S(1)}) custom-call(s32[2,16]{1,0:T(2,128)S(1)} %bitcast.10, s32[1]{0:T(128)} %bitcast.6.load, bf16[16,256,256]{2,1,0:T(8,128)(2,1)S(1)} %bitcast.8, f32[2,4,768,128]{3,2,1,0:T(8,128)S(1)} %get-tuple-element.10.ext.old, f32[2,256,256]{2,1,0:T(8,128)S(1)} %get-tuple-element.11.probe, ...), custom_call_target="tpu_custom_call" | custom-call | tf_op jit(solution)/shard_map/pallas_call | solution.py:107
  101.9 36.7 %shard_map.90 = (f32[2,256,256]{2,1,0:T(8,128)S(1)}, f32[2,256,256]{2,1,0:T(8,128)S(1)}) custom-call(f32[3,4,768,128]{3,2,1,0:T(8,128)S(1)} %get-tuple-element.12.grad, f32[3,256,256]{2,1,0:T(8,128)S(1)} %get-tuple-element.13.psum, f32[2,4,768,128]{3,2,1,0:T(8,128)S(1)} %get-tuple-element.10.ext.old, f32[2,256,256]{2,1,0:T(8,128)S(1)} %get-tuple-element.11.probe), custom_call_target="tpu_custom_call" | custom-call | tf_op jit(solution)/shard_map/pallas_call | solution.py:398
  138.6 0.8 copy.12
  139.4 0.8 copy.13
Async XLA Ops:
  0.6 27.4 %copy-start.2 = (bf16[512,512]{1,0:T(8,128)(2,1)S(1)}, bf16[512,512]{1,0:T(8,128)(2,1)}, u32[]{:S(2)}) copy-start(bf16[512,512]{1,0:T(8,128)(2,1)} %constant.5.clone.inv) | copy-start | bytes 1572868
  0.6 27.4 %copy-start.3 = (bf16[512,512]{1,0:T(8,128)(2,1)S(1)}, bf16[512,512]{1,0:T(8,128)(2,1)}, u32[]{:S(2)}) copy-start(bf16[512,512]{1,0:T(8,128)(2,1)} %constant.4.clone.fwd) | copy-start | bytes 1572868
  0.7 27.4 %copy-start.1 = (f32[2,256,256]{2,1,0:T(8,128)S(1)}, f32[2,256,256]{2,1,0:T(8,128)}, u32[]{:S(2)}) copy-start(f32[2,256,256]{2,1,0:T(8,128)} %probe.3) | copy-start | bytes 1572868
  0.7 27.4 %copy-start = (bf16[1,1,16,256,256]{4,3,2,1,0:T(8,128)(2,1)S(1)}, bf16[1,1,16,256,256]{4,3,2,1,0:T(8,128)(2,1)}, u32[]{:S(2)}) copy-start(bf16[1,1,16,256,256]{4,3,2,1,0:T(8,128)(2,1)} %param.9) | copy-start | bytes 6291460
  1.5 1.3 copy-start.4
  2.8 25.3 %copy-start.5 = (s32[1,1,16,2]{2,3,1,0:T(2,128)S(1)}, s32[1,1,16,2]{2,3,1,0:T(2,128)}, u32[]{:S(2)}) copy-start(s32[1,1,16,2]{2,3,1,0:T(2,128)} %param.7) | copy-start | bytes 388

commit v7 on v6

--- a/solution.py
+++ b/solution.py
@@ -202,21 +202,55 @@
 BOTH = pl.ds(1, 2)
 
 
-def send_halo(send, at, ext):
+def send_halo(send, at, ext, relay):
     near, far = pl.ds(at.near_edge, 1), pl.ds(at.far_edge, 1)
     there_near, there_far = pl.ds(at.far_rim, 1), pl.ds(at.near_rim, 1)
     up, down, aside = (at.above, at.below), (at.below, at.above), (at.aside, at.aside)
     up_aside, down_aside = (at.above & at.aside, at.below & at.aside), (at.below & at.aside, at.above & at.aside)
-    return [
-        send(ext.at[:, far, INNER, :], ext.at[:, there_far, INNER, :], at.far, *aside),
-        send(ext.at[:, BOTH, TOP, :], ext.at[:, BOTH, BELOW, :], at.up, *up),
-        send(ext.at[:, BOTH, BOTTOM, :], ext.at[:, BOTH, ABOVE, :], at.down, *down),
-        send(ext.at[:, far, TOP, :], ext.at[:, there_far, BELOW, :], at.far_north, *up_aside),
-        send(ext.at[:, far, BOTTOM, :], ext.at[:, there_far, ABOVE, :], at.far_south, *down_aside),
+    up_near = (at.above & ~at.over, at.below & ~at.under)
+    down_near = (at.below & ~at.under, at.above & ~at.over)
+    real, imag = pl.ds(0, 1), pl.ds(1, 1)
+    relays = [
+        send(ext.at[:, near, TOP, :], relay, at.row_first, at.over, at.first),
+        send(ext.at[:, near, BOTTOM, :], relay, at.row_final, at.under, at.final),
+    ]
+    side = [send(ext.at[imag, far, INNER, :], ext.at[imag, there_far, INNER, :], at.far, *aside)]
+    strips = [
+        send(ext.at[:, near, TOP, :], ext.at[:, near, BELOW, :], at.up, *up_near),
+        send(ext.at[:, near, BOTTOM, :], ext.at[:, near, ABOVE, :], at.down, *down_near),
+    ]
+    rest = [
+        send(ext.at[real, far, INNER, :], ext.at[real, there_far, INNER, :], at.far, *aside),
+        send(ext.at[:, far, TOP, :], ext.at[:, far, BELOW, :], at.up, *up),
+        send(ext.at[:, far, BOTTOM, :], ext.at[:, far, ABOVE, :], at.down, *down),
+        send(ext.at[real, far, TOP, :], ext.at[real, there_far, BELOW, :], at.far_north, *up_aside),
+        send(ext.at[real, far, BOTTOM, :], ext.at[real, there_far, ABOVE, :], at.far_south, *down_aside),
         send(ext.at[:, near, INNER, :], ext.at[:, there_near, INNER, :], at.twin),
-        send(ext.at[:, near, TOP, :], ext.at[:, there_near, BELOW, :], at.near_north, *up),
-        send(ext.at[:, near, BOTTOM, :], ext.at[:, there_near, ABOVE, :], at.near_south, *down),
-    ]
+    ]
+    return (relays, side, strips), rest
+
+
+def pass_on_halo(send, at, ext, relay, arriving):
+    relays, side, strips = arriving
+    near, far, there = pl.ds(at.near_edge, 1), pl.ds(at.far_rim, 1), pl.ds(at.far_rim, 1)
+    imag = pl.ds(1, 1)
+    up_aside, down_aside = (at.above & at.aside, at.below & at.aside), (at.below & at.aside, at.above & at.aside)
+    copies, relayed = [], []
+    arrive(relays)
+    for (row, col), rows, sends, gets in (
+        (at.row_under, BELOW, at.first, at.under),
+        (at.row_over, ABOVE, at.final, at.over),
+    ):
+        relayed.append(send(relay, ext.at[:, near, rows, :], (row, col), sends, gets))
+    arrive(side)
+    copies += [
+        send(ext.at[imag, far, TOP, :], ext.at[imag, far, BELOW, :], at.up, *up_aside),
+        send(ext.at[imag, far, BOTTOM, :], ext.at[imag, far, ABOVE, :], at.down, *down_aside),
+    ]
+    arrive(strips + relayed)
+    for rows, has in ((ABOVE, at.above), (BELOW, at.below)):
+        copies.append(send(ext.at[:, near, rows, :], ext.at[:, there, rows, :], at.twin, has, has))
+    return copies
 
 
 def clear_outside(at, ext):
@@ -239,21 +273,23 @@
         ext[:, 3, : 2 * F, :] = jnp.zeros((2, 2 * F, 128), f32)
 
 
-def open_kernel(cells, ext, send_sem, recv_sem):
+def open_kernel(cells, ext, relay, send_sem, recv_sem):
     at = Places()
-    meet(at.around)
+    meet((*at.around, *at.along_y[::2], *at.along_z[::2]))
     for part in range(2):
         for j in range(2):
             ext[part, 1 + j, TILE, :] = cells[part, :, 128 * j : 128 * j + 128]
     send = Sender(send_sem, recv_sem)
-    arrive(send_halo(send, at, ext))
+    arriving, halo = send_halo(send, at, ext, relay)
+    halo += pass_on_halo(send, at, ext, relay, arriving)
+    arrive(halo)
     send.close()
     clear_outside(at, ext)
 
 
 def step_kernel(last, grad, psum, old, probe, new, probe_new, *scratch):
-    from_up, from_down, sides_in, far_in, side, strips, relay = scratch[:7]
-    acc0, buf0, acc1, buf1, acc2, buf2, buf3, send_sem, recv_sem = scratch[7:]
+    from_up, from_down, sides_in, far_in, side, strips, relay, halo_relay = scratch[:8]
+    acc0, buf0, acc1, buf1, acc2, buf2, buf3, send_sem, recv_sem = scratch[8:]
     at = Places()
     meet((*at.around, *at.along_x, *at.along_y, *at.along_z))
     send = Sender(send_sem, recv_sem)
@@ -358,10 +394,13 @@
     s4 = [send(part, part, peer) for peer in at.along_y]
     if not last:
         finish_object()
-        halo = send_halo(send, at, new)
+        arriving, halo = send_halo(send, at, new, halo_relay)
     arrive(s4)
     part = probe_new.at[:, pl.ds(base_x, 32), :]
-    arrive([send(part, part, peer) for peer in at.along_x])
+    s5 = [send(part, part, peer) for peer in at.along_x]
+    if not last:
+        halo += pass_on_halo(send, at, new, halo_relay, arriving)
+    arrive(s5)
     part = probe_new.at[:, pl.ds(base, 128), :]
     s6 = send(part, part, at.twin)
     if last:
@@ -385,7 +424,11 @@
         out_shape=jax.ShapeDtypeStruct((2, 4, ROWS, 128), f32),
         in_specs=[VMEM],
         out_specs=VMEM,
-        scratch_shapes=[pltpu.SemaphoreType.DMA((8,)), pltpu.SemaphoreType.DMA((8,))],
+        scratch_shapes=[
+            pltpu.VMEM((2, 1, HALF, 128), f32),
+            pltpu.SemaphoreType.DMA((20,)),
+            pltpu.SemaphoreType.DMA((20,)),
+        ],
         compiler_params=pltpu.CompilerParams(
             collective_id=0, has_side_effects=True, vmem_limit_bytes=LIMIT
         ),
@@ -394,7 +437,7 @@
 
 def step(last, grad, psum, old, probe):
     shape = (2, F, F) if last else (2, 4, ROWS, 128)
-    copies = 29 if last else 37
+    copies = 29 if last else 49
     return pl.pallas_call(
         functools.partial(step_kernel, last),
         out_shape=(jax.ShapeDtypeStruct(shape, f32), jax.ShapeDtypeStruct((2, F, F), f32)),
@@ -408,6 +451,7 @@
             pltpu.VMEM((3, 1, F, 128), f32),
             pltpu.VMEM((2, 3, 1, HALF, 128), f32),
             pltpu.VMEM((3, 1, HALF, 128), f32),
+            pltpu.VMEM((2, 1, HALF, 128), f32),
             pltpu.VMEM((3, 128, F), f32),
             pltpu.VMEM((3, 128, F), f32),
             pltpu.VMEM((3, 32, F), f32),

time: 140 us -> 135 us (0.964)
  Pallas kernels: 136 us -> 131 us
    pallas_call x1, Pallas kernels: 25.3 us -> 19.2 us  [open_halo(): pl.pallas_call(open_kernel, out_shape=jax.ShapeDtypeStruct((2, 4, ROWS, 1...]
where the time goes in v7:
time: 135 us
  Pallas kernels  131 us (97%)
  local copies, waits for them, and re-layouts  2.93 us (2%)
  between operations  1.55 us (1%)
    pallas_call x2, Pallas kernels, step(): pl.pallas_call(functools.partial(step_kernel, last), out_shape=(jax.Shape...  78 us
    pallas_call x2, Pallas kernels, slots(): pl.pallas_call(slots_kernel, out_shape=(jax.ShapeDtypeStruct((3, 4, ROWS,...  33.5 us
    pallas_call x1, Pallas kernels, open_halo(): pl.pallas_call(open_kernel, out_shape=jax.ShapeDtypeStruct((2, 4, ROWS, 1...  19.2 us
    unnamed x14, local copies, waits for them, and re-layouts  2.93 us

profile of v7, /device:TPU:1, one launch (start us, length us, event | category | flops | bytes accessed | tf_op | source)
XLA Modules:
  0.0 135.2 jit_solution(16201771598122143630)
XLA Ops:
  0.6 0.0 copy-start.2
  0.6 0.0 copy-start.3
  0.7 0.0 copy-start.1
  0.7 0.0 copy-start
  1.5 0.0 copy-start.4
  1.5 1.3 copy-done.4
  2.8 0.0 copy-start.5
  2.8 19.2 %shard_map.86.ext.old = f32[2,4,768,128]{3,2,1,0:T(8,128)S(1)} custom-call(f32[2,256,256]{2,1,0:T(8,128)S(1)} %copy-done.4), custom_call_target="tpu_custom_call" | custom-call | tf_op jit(solution)/shard_map/pallas_call | solution.py:422
  22.0 0.0 copy-done.2
  22.0 0.0 copy-done.3
  22.0 0.0 copy-done.1
  22.0 0.0 copy-done
  22.0 0.0 copy-done.5
  22.0 16.7 %shard_map.87 = (f32[3,4,768,128]{3,2,1,0:T(8,128)S(1)}, f32[3,256,256]{2,1,0:T(8,128)S(1)}) custom-call(s32[2,16]{1,0:T(2,128)S(1)} %bitcast.9, s32[1]{0:T(128)} %bitcast.5.load, bf16[16,256,256]{2,1,0:T(8,128)(2,1)S(1)} %bitcast.7, f32[2,4,768,128]{3,2,1,0:T(8,128)S(1)} %shard_map.86.ext.old, f32[2,256,256]{2,1,0:T(8,128)S(1)} %copy-done.1, ...), custom_call_target="tpu_custom_call" | custom-call | tf_op jit(solution)/shard_map/pallas_call | solution.py:107
  38.8 41.5 %shard_map.88 = (f32[2,4,768,128]{3,2,1,0:T(8,128)S(1)}, f32[2,256,256]{2,1,0:T(8,128)S(1)}) custom-call(f32[3,4,768,128]{3,2,1,0:T(8,128)S(1)} %get-tuple-element.8.grad, f32[3,256,256]{2,1,0:T(8,128)S(1)} %get-tuple-element.9.psum, f32[2,4,768,128]{3,2,1,0:T(8,128)S(1)} %shard_map.86.ext.old, f32[2,256,256]{2,1,0:T(8,128)S(1)} %copy-done.1), custom_call_target="tpu_custom_call" | custom-call | tf_op jit(solution)/shard_map/pallas_call | solution.py:441
  80.3 16.8 %shard_map.89 = (f32[3,4,768,128]{3,2,1,0:T(8,128)S(1)}, f32[3,256,256]{2,1,0:T(8,128)S(1)}) custom-call(s32[2,16]{1,0:T(2,128)S(1)} %bitcast.10, s32[1]{0:T(128)} %bitcast.6.load, bf16[16,256,256]{2,1,0:T(8,128)(2,1)S(1)} %bitcast.8, f32[2,4,768,128]{3,2,1,0:T(8,128)S(1)} %get-tuple-element.10.ext.old, f32[2,256,256]{2,1,0:T(8,128)S(1)} %get-tuple-element.11.probe, ...), custom_call_target="tpu_custom_call" | custom-call | tf_op jit(solution)/shard_map/pallas_call | solution.py:107
  97.0 36.6 %shard_map.90 = (f32[2,256,256]{2,1,0:T(8,128)S(1)}, f32[2,256,256]{2,1,0:T(8,128)S(1)}) custom-call(f32[3,4,768,128]{3,2,1,0:T(8,128)S(1)} %get-tuple-element.12.grad, f32[3,256,256]{2,1,0:T(8,128)S(1)} %get-tuple-element.13.psum, f32[2,4,768,128]{3,2,1,0:T(8,128)S(1)} %get-tuple-element.10.ext.old, f32[2,256,256]{2,1,0:T(8,128)S(1)} %get-tuple-element.11.probe), custom_call_target="tpu_custom_call" | custom-call | tf_op jit(solution)/shard_map/pallas_call | solution.py:441
  133.6 0.8 copy.12
  134.4 0.8 copy.13
Async XLA Ops:
  0.6 21.4 %copy-start.2 = (bf16[512,512]{1,0:T(8,128)(2,1)S(1)}, bf16[512,512]{1,0:T(8,128)(2,1)}, u32[]{:S(2)}) copy-start(bf16[512,512]{1,0:T(8,128)(2,1)} %constant.5.clone.inv) | copy-start | bytes 1572868
  0.6 21.4 %copy-start.3 = (bf16[512,512]{1,0:T(8,128)(2,1)S(1)}, bf16[512,512]{1,0:T(8,128)(2,1)}, u32[]{:S(2)}) copy-start(bf16[512,512]{1,0:T(8,128)(2,1)} %constant.4.clone.fwd) | copy-start | bytes 1572868
  0.7 21.4 %copy-start.1 = (f32[2,256,256]{2,1,0:T(8,128)S(1)}, f32[2,256,256]{2,1,0:T(8,128)}, u32[]{:S(2)}) copy-start(f32[2,256,256]{2,1,0:T(8,128)} %probe.3) | copy-start | bytes 1572868
  0.7 21.4 %copy-start = (bf16[1,1,16,256,256]{4,3,2,1,0:T(8,128)(2,1)S(1)}, bf16[1,1,16,256,256]{4,3,2,1,0:T(8,128)(2,1)}, u32[]{:S(2)}) copy-start(bf16[1,1,16,256,256]{4,3,2,1,0:T(8,128)(2,1)} %param.9) | copy-start | bytes 6291460
  1.5 1.3 copy-start.4
  2.8 19.2 %copy-start.5 = (s32[1,1,16,2]{2,3,1,0:T(2,128)S(1)}, s32[1,1,16,2]{2,3,1,0:T(2,128)}, u32[]{:S(2)}) copy-start(s32[1,1,16,2]{2,3,1,0:T(2,128)} %param.7) | copy-start | bytes 388

commit v8 on v7

--- a/solution.py
+++ b/solution.py
@@ -202,38 +202,43 @@
 BOTH = pl.ds(1, 2)
 
 
-def send_halo(send, at, ext, relay):
-    near, far = pl.ds(at.near_edge, 1), pl.ds(at.far_edge, 1)
-    there_near, there_far = pl.ds(at.far_rim, 1), pl.ds(at.near_rim, 1)
+def send_far_halo(send, at, ext):
+    far, there = pl.ds(at.far_edge, 1), pl.ds(at.near_rim, 1)
     up, down, aside = (at.above, at.below), (at.below, at.above), (at.aside, at.aside)
     up_aside, down_aside = (at.above & at.aside, at.below & at.aside), (at.below & at.aside, at.above & at.aside)
+    real, imag = pl.ds(0, 1), pl.ds(1, 1)
+    return [send(ext.at[imag, far, INNER, :], ext.at[imag, there, INNER, :], at.far, *aside)], [
+        send(ext.at[real, far, INNER, :], ext.at[real, there, INNER, :], at.far, *aside),
+        send(ext.at[:, far, TOP, :], ext.at[:, far, BELOW, :], at.up, *up),
+        send(ext.at[:, far, BOTTOM, :], ext.at[:, far, ABOVE, :], at.down, *down),
+        send(ext.at[real, far, TOP, :], ext.at[real, there, BELOW, :], at.far_north, *up_aside),
+        send(ext.at[real, far, BOTTOM, :], ext.at[real, there, ABOVE, :], at.far_south, *down_aside),
+    ]
+
+
+def send_near_halo(send, at, ext, relay):
+    near, there = pl.ds(at.near_edge, 1), pl.ds(at.far_rim, 1)
+    up, down = (at.above, at.below), (at.below, at.above)
     up_near = (at.above & ~at.over, at.below & ~at.under)
     down_near = (at.below & ~at.under, at.above & ~at.over)
     real, imag = pl.ds(0, 1), pl.ds(1, 1)
     relays = [
-        send(ext.at[:, near, TOP, :], relay, at.row_first, at.over, at.first),
-        send(ext.at[:, near, BOTTOM, :], relay, at.row_final, at.under, at.final),
-    ]
-    side = [send(ext.at[imag, far, INNER, :], ext.at[imag, there_far, INNER, :], at.far, *aside)]
+        send(ext.at[real, near, TOP, :], relay, at.row_first, at.over, at.first),
+        send(ext.at[real, near, BOTTOM, :], relay, at.row_final, at.under, at.final),
+    ]
     strips = [
-        send(ext.at[:, near, TOP, :], ext.at[:, near, BELOW, :], at.up, *up_near),
-        send(ext.at[:, near, BOTTOM, :], ext.at[:, near, ABOVE, :], at.down, *down_near),
-    ]
-    rest = [
-        send(ext.at[real, far, INNER, :], ext.at[real, there_far, INNER, :], at.far, *aside),
-        send(ext.at[:, far, TOP, :], ext.at[:, far, BELOW, :], at.up, *up),
-        send(ext.at[:, far, BOTTOM, :], ext.at[:, far, ABOVE, :], at.down, *down),
-        send(ext.at[real, far, TOP, :], ext.at[real, there_far, BELOW, :], at.far_north, *up_aside),
-        send(ext.at[real, far, BOTTOM, :], ext.at[real, there_far, ABOVE, :], at.far_south, *down_aside),
-        send(ext.at[:, near, INNER, :], ext.at[:, there_near, INNER, :], at.twin),
-    ]
-    return (relays, side, strips), rest
+        send(ext.at[imag, near, TOP, :], ext.at[imag, near, BELOW, :], at.up, *up),
+        send(ext.at[imag, near, BOTTOM, :], ext.at[imag, near, ABOVE, :], at.down, *down),
+        send(ext.at[real, near, TOP, :], ext.at[real, near, BELOW, :], at.up, *up_near),
+        send(ext.at[real, near, BOTTOM, :], ext.at[real, near, ABOVE, :], at.down, *down_near),
+    ]
+    return relays, strips, [send(ext.at[:, near, INNER, :], ext.at[:, there, INNER, :], at.twin)]
 
 
 def pass_on_halo(send, at, ext, relay, arriving):
     relays, side, strips = arriving
     near, far, there = pl.ds(at.near_edge, 1), pl.ds(at.far_rim, 1), pl.ds(at.far_rim, 1)
-    imag = pl.ds(1, 1)
+    real, imag = pl.ds(0, 1), pl.ds(1, 1)
     up_aside, down_aside = (at.above & at.aside, at.below & at.aside), (at.below & at.aside, at.above & at.aside)
     copies, relayed = [], []
     arrive(relays)
@@ -241,7 +246,7 @@
         (at.row_under, BELOW, at.first, at.under),
         (at.row_over, ABOVE, at.final, at.over),
     ):
-        relayed.append(send(relay, ext.at[:, near, rows, :], (row, col), sends, gets))
+        relayed.append(send(relay, ext.at[real, near, rows, :], (row, col), sends, gets))
     arrive(side)
     copies += [
         send(ext.at[imag, far, TOP, :], ext.at[imag, far, BELOW, :], at.up, *up_aside),
@@ -280,8 +285,9 @@
         for j in range(2):
             ext[part, 1 + j, TILE, :] = cells[part, :, 128 * j : 128 * j + 128]
     send = Sender(send_sem, recv_sem)
-    arriving, halo = send_halo(send, at, ext, relay)
-    halo += pass_on_halo(send, at, ext, relay, arriving)
+    relays, strips, rest = send_near_halo(send, at, ext, relay)
+    side, halo = send_far_halo(send, at, ext)
+    halo += rest + pass_on_halo(send, at, ext, relay, (relays, side, strips))
     arrive(halo)
     send.close()
     clear_outside(at, ext)
@@ -295,7 +301,6 @@
     send = Sender(send_sem, recv_sem)
     above, below = at.above, at.below
     up, down = (above, below), (below, above)
-    before, after = at.col > 0, at.col < at.n_col - 1
     base = at.core * 128
     base_x = base + at.x * 32
     base_y = base_x + at.y * 8
@@ -306,9 +311,13 @@
     s0 = send(psum.at[:, pl.ds(128 - base, 128), :], buf0, at.twin)
     twins = send(grad.at[:, near_rim, : 2 * F, :], sides_in.at[at.core], at.twin)
     corners = [
-        send(grad.at[:, far_rim, ABOVE, :], far_in.at[1], at.up, *up),
-        send(grad.at[:, far_rim, BELOW, :], far_in.at[0], at.down, *down),
-    ]
+        [
+            send(grad.at[pl.ds(ch, 1), far_rim, ABOVE, :], far_in.at[1, pl.ds(ch, 1)], at.up, *up),
+            send(grad.at[pl.ds(ch, 1), far_rim, BELOW, :], far_in.at[0, pl.ds(ch, 1)], at.down, *down),
+        ]
+        for ch in range(3)
+    ]
+    near_rims = []
     rims = [
         send(grad.at[:, far_edge, ABOVE, :], from_down.at[:, far_part], at.up, *up),
         send(grad.at[:, far_edge, BELOW, :], from_up.at[:, far_part], at.down, *down),
@@ -330,7 +339,7 @@
     ]
 
     def send_near():
-        rims.extend([
+        near_rims.extend([
             send(strips.at[0], from_down.at[:, near_part], at.up, above & ~at.over, below & ~at.under),
             send(strips.at[1], from_up.at[:, near_part], at.down, below & ~at.under, above & ~at.over),
         ])
@@ -338,14 +347,12 @@
     if not last:
         send_near()
 
-    def send_side():
-        rims.append(send(side, sides_in.at[1 - at.core, :, :, INNER, :], at.far, at.aside, at.aside))
-
-    arrive(corners)
     for ch in range(3):
+        arrive(corners[ch])
         side[ch, 0, :HALF, :] = grad[ch, at.far_rim, TOP, :] + jnp.where(above, far_in[0, ch, 0], 0.0)
         side[ch, 0, HALF:, :] = grad[ch, at.far_rim, BOTTOM, :] + jnp.where(below, far_in[1, ch, 0], 0.0)
-    send_side()
+        there = sides_in.at[1 - at.core, pl.ds(ch, 1), :, INNER, :]
+        rims.append(send(side.at[pl.ds(ch, 1)], there, at.far, at.aside, at.aside))
     arrive(s1)
     acc1[...] = acc0[:, pl.ds(at.x * 32, 32), :] + buf1[0] + buf1[1] + buf1[2]
     s2 = [
@@ -360,31 +367,35 @@
     s3 = [send(acc2, buf3.at[at.z], at.along_z[d - 1]) for d in (1, 2, 3)]
 
     arrive(relays)
-    rims += [
+    near_rims += [
         send(relay, from_down.at[:, near_part], at.row_under, at.first, at.under),
         send(relay, from_up.at[:, near_part], at.row_over, at.final, at.over),
     ]
 
-    def finish_object():
+    def finish(tile, beside):
+        for half, (level, rim) in enumerate(((above, from_up), (below, from_down))):
+            rows = pl.ds(HALF * half, HALF)
+            place = pl.ds(HALF + HALF * half, HALF)
+            sums = []
+            for ch in range(3):
+                rims_sum = jnp.where(level, rim[ch, tile - 1], 0.0) + beside(ch, place)
+                sums.append(grad[ch, tile, place, :] + rims_sum)
+            share = 1.0 / (sums[2] + 1.0)
+            for part in range(2):
+                cells = old[part, tile, place, :] - sums[part] * share
+                if last:
+                    columns = pl.ds(pl.multiple_of(128 * (tile - 1), 128), 128)
+                    new[part, rows, columns] = cells
+                else:
+                    new[part, tile, place, :] = cells
+
+    def finish_far():
         arrive(rims)
-        for j, beside in enumerate((before, after)):
-            for half, (level, rim) in enumerate(((above, from_up), (below, from_down))):
-                rows = pl.ds(HALF * half, HALF)
-                place = pl.ds(HALF + HALF * half, HALF)
-                sums = []
-                for ch in range(3):
-                    sums.append(
-                        grad[ch, 1 + j, place, :]
-                        + jnp.where(level, rim[ch, j], 0.0)
-                        + jnp.where(beside, sides_in[j, ch, 0, place, :], 0.0)
-                    )
-                weight = sums[2] + 1.0
-                for part in range(2):
-                    cells = old[part, 1 + j, place, :] - sums[part] / weight
-                    if last:
-                        new[part, rows, 128 * j : 128 * j + 128] = cells
-                    else:
-                        new[part, 1 + j, place, :] = cells
+        finish(at.far_edge, lambda ch, place: jnp.where(at.aside, sides_in[at.core, ch, 0, place, :], 0.0))
+
+    def finish_near():
+        arrive(near_rims)
+        finish(at.near_edge, lambda ch, place: sides_in[1 - at.core, ch, 0, place, :])
 
     arrive(s3)
     total = buf3[0] + buf3[1] + buf3[2] + buf3[3]
@@ -393,8 +404,11 @@
     part = probe_new.at[:, mine, :]
     s4 = [send(part, part, peer) for peer in at.along_y]
     if not last:
-        finish_object()
-        arriving, halo = send_halo(send, at, new, halo_relay)
+        finish_far()
+        passing, halo = send_far_halo(send, at, new)
+        finish_near()
+        relays, strips_out, rest = send_near_halo(send, at, new, halo_relay)
+        arriving, halo = (relays, passing, strips_out), halo + rest
     arrive(s4)
     part = probe_new.at[:, pl.ds(base_x, 32), :]
     s5 = [send(part, part, peer) for peer in at.along_x]
@@ -404,7 +418,8 @@
     part = probe_new.at[:, pl.ds(base, 128), :]
     s6 = send(part, part, at.twin)
     if last:
-        finish_object()
+        finish_far()
+        finish_near()
     arrive([s6])
     if not last:
         arrive(halo)
@@ -425,9 +440,9 @@
         in_specs=[VMEM],
         out_specs=VMEM,
         scratch_shapes=[
-            pltpu.VMEM((2, 1, HALF, 128), f32),
-            pltpu.SemaphoreType.DMA((20,)),
-            pltpu.SemaphoreType.DMA((20,)),
+            pltpu.VMEM((1, 1, HALF, 128), f32),
+            pltpu.SemaphoreType.DMA((22,)),
+            pltpu.SemaphoreType.DMA((22,)),
         ],
         compiler_params=pltpu.CompilerParams(
             collective_id=0, has_side_effects=True, vmem_limit_bytes=LIMIT
@@ -437,7 +452,7 @@
 
 def step(last, grad, psum, old, probe):
     shape = (2, F, F) if last else (2, 4, ROWS, 128)
-    copies = 29 if last else 49
+    copies = 35 if last else 57
     return pl.pallas_call(
         functools.partial(step_kernel, last),
         out_shape=(jax.ShapeDtypeStruct(shape, f32), jax.ShapeDtypeStruct((2, F, F), f32)),
@@ -451,7 +466,7 @@
             pltpu.VMEM((3, 1, F, 128), f32),
             pltpu.VMEM((2, 3, 1, HALF, 128), f32),
             pltpu.VMEM((3, 1, HALF, 128), f32),
-            pltpu.VMEM((2, 1, HALF, 128), f32),
+            pltpu.VMEM((1, 1, HALF, 128), f32),
             pltpu.VMEM((3, 128, F), f32),
             pltpu.VMEM((3, 128, F), f32),
             pltpu.VMEM((3, 32, F), f32),

time: 135 us -> 136 us (level)
    pallas_call x2, Pallas kernels: 33.5 us -> 11.3 us  [slots(): pl.pallas_call(slots_kernel, out_shape=(jax.ShapeDtypeStruct((3, 4, ROWS,...]
    pallas_call x2, Pallas kernels: 78 us -> 99.5 us  [step(): pl.pallas_call(functools.partial(step_kernel, last), out_shape=(jax.Shape...]
    pallas_call x1, Pallas kernels: 19.2 us -> 20.6 us  [open_halo(): pl.pallas_call(open_kernel, out_shape=jax.ShapeDtypeStruct((2, 4, ROWS, 1...]
where the time goes in v8:
time: 136 us
  Pallas kernels  131 us (96%)
  local copies, waits for them, and re-layouts  2.93 us (2%)
  between operations  1.55 us (1%)
    pallas_call x2, Pallas kernels, step(): pl.pallas_call(functools.partial(step_kernel, last), out_shape=(jax.Shape...  99.5 us
    pallas_call x1, Pallas kernels, open_halo(): pl.pallas_call(open_kernel, out_shape=jax.ShapeDtypeStruct((2, 4, ROWS, 1...  20.6 us
    pallas_call x2, Pallas kernels, slots(): pl.pallas_call(slots_kernel, out_shape=(jax.ShapeDtypeStruct((3, 4, ROWS,...  11.3 us
    unnamed x14, local copies, waits for them, and re-layouts  2.93 us

profile of v8, /device:TPU:1, one launch (start us, length us, event | category | flops | bytes accessed | tf_op | source)
XLA Modules:
  0.0 135.9 jit_solution(3035778770137098846)
XLA Ops:
  0.6 0.0 copy-start.2
  0.6 0.0 copy-start.3
  0.7 0.0 copy-start.1
  0.7 0.0 copy-start
  1.5 0.0 copy-start.4
  1.5 1.3 copy-done.4
  2.8 0.0 copy-start.5
  2.8 20.6 %shard_map.86.ext.old = f32[2,4,768,128]{3,2,1,0:T(8,128)S(1)} custom-call(f32[2,256,256]{2,1,0:T(8,128)S(1)} %copy-done.4), custom_call_target="tpu_custom_call" | custom-call | tf_op jit(solution)/shard_map/pallas_call | solution.py:437
  23.4 0.0 copy-done.2
  23.4 0.0 copy-done.3
  23.5 0.0 copy-done.1
  23.5 0.0 copy-done
  23.5 0.0 copy-done.5
  23.5 5.7 %shard_map.87 = (f32[3,4,768,128]{3,2,1,0:T(8,128)S(1)}, f32[3,256,256]{2,1,0:T(8,128)S(1)}) custom-call(s32[2,16]{1,0:T(2,128)S(1)} %bitcast.9, s32[1]{0:T(128)} %bitcast.5.load, bf16[16,256,256]{2,1,0:T(8,128)(2,1)S(1)} %bitcast.7, f32[2,4,768,128]{3,2,1,0:T(8,128)S(1)} %shard_map.86.ext.old, f32[2,256,256]{2,1,0:T(8,128)S(1)} %copy-done.1, ...), custom_call_target="tpu_custom_call" | custom-call | tf_op jit(solution)/shard_map/pallas_call | solution.py:107
  29.1 49.9 %shard_map.88 = (f32[2,4,768,128]{3,2,1,0:T(8,128)S(1)}, f32[2,256,256]{2,1,0:T(8,128)S(1)}) custom-call(f32[3,4,768,128]{3,2,1,0:T(8,128)S(1)} %get-tuple-element.8.grad, f32[3,256,256]{2,1,0:T(8,128)S(1)} %get-tuple-element.9.psum, f32[2,4,768,128]{3,2,1,0:T(8,128)S(1)} %shard_map.86.ext.old, f32[2,256,256]{2,1,0:T(8,128)S(1)} %copy-done.1), custom_call_target="tpu_custom_call" | custom-call | tf_op jit(solution)/shard_map/pallas_call | solution.py:456
  79.1 5.7 %shard_map.89 = (f32[3,4,768,128]{3,2,1,0:T(8,128)S(1)}, f32[3,256,256]{2,1,0:T(8,128)S(1)}) custom-call(s32[2,16]{1,0:T(2,128)S(1)} %bitcast.10, s32[1]{0:T(128)} %bitcast.6.load, bf16[16,256,256]{2,1,0:T(8,128)(2,1)S(1)} %bitcast.8, f32[2,4,768,128]{3,2,1,0:T(8,128)S(1)} %get-tuple-element.10.ext.old, f32[2,256,256]{2,1,0:T(8,128)S(1)} %get-tuple-element.11.probe, ...), custom_call_target="tpu_custom_call" | custom-call | tf_op jit(solution)/shard_map/pallas_call | solution.py:107
  84.7 49.6 %shard_map.90 = (f32[2,256,256]{2,1,0:T(8,128)S(1)}, f32[2,256,256]{2,1,0:T(8,128)S(1)}) custom-call(f32[3,4,768,128]{3,2,1,0:T(8,128)S(1)} %get-tuple-element.12.grad, f32[3,256,256]{2,1,0:T(8,128)S(1)} %get-tuple-element.13.psum, f32[2,4,768,128]{3,2,1,0:T(8,128)S(1)} %get-tuple-element.10.ext.old, f32[2,256,256]{2,1,0:T(8,128)S(1)} %get-tuple-element.11.probe), custom_call_target="tpu_custom_call" | custom-call | tf_op jit(solution)/shard_map/pallas_call | solution.py:456
  134.4 0.8 copy.12
  135.2 0.8 copy.13
Async XLA Ops:
  0.6 22.8 %copy-start.2 = (bf16[512,512]{1,0:T(8,128)(2,1)S(1)}, bf16[512,512]{1,0:T(8,128)(2,1)}, u32[]{:S(2)}) copy-start(bf16[512,512]{1,0:T(8,128)(2,1)} %constant.5.clone.inv) | copy-start | bytes 1572868
  0.6 22.8 %copy-start.3 = (bf16[512,512]{1,0:T(8,128)(2,1)S(1)}, bf16[512,512]{1,0:T(8,128)(2,1)}, u32[]{:S(2)}) copy-start(bf16[512,512]{1,0:T(8,128)(2,1)} %constant.4.clone.fwd) | copy-start | bytes 1572868
  0.7 22.8 %copy-start.1 = (f32[2,256,256]{2,1,0:T(8,128)S(1)}, f32[2,256,256]{2,1,0:T(8,128)}, u32[]{:S(2)}) copy-start(f32[2,256,256]{2,1,0:T(8,128)} %probe.3) | copy-start | bytes 1572868
  0.7 22.8 %copy-start = (bf16[1,1,16,256,256]{4,3,2,1,0:T(8,128)(2,1)S(1)}, bf16[1,1,16,256,256]{4,3,2,1,0:T(8,128)(2,1)}, u32[]{:S(2)}) copy-start(bf16[1,1,16,256,256]{4,3,2,1,0:T(8,128)(2,1)} %param.9) | copy-start | bytes 6291460
  1.5 1.3 copy-start.4
  2.8 20.7 %copy-start.5 = (s32[1,1,16,2]{2,3,1,0:T(2,128)S(1)}, s32[1,1,16,2]{2,3,1,0:T(2,128)}, u32[]{:S(2)}) copy-start(s32[1,1,16,2]{2,3,1,0:T(2,128)} %param.7) | copy-start | bytes 388

commit v9 on v8

--- a/solution.py
+++ b/solution.py
@@ -19,17 +19,16 @@
     return jnp.asarray(fwd,bf16), jnp.asarray(inv,bf16)
 
 CH=16; B=2; ROWS=3*F
-def both_sides(table, other, cells):
-    re = jnp.dot(table[:F, :], cells[...], preferred_element_type=f32).astype(bf16)
-    im = jnp.dot(table[F:, :], cells[...], preferred_element_type=f32).astype(bf16)
-    stacked = jnp.concatenate(
-        [jnp.concatenate([re[:, F * b : F * b + F], im[:, F * b : F * b + F]], 1) for b in range(B)], 0
-    )
-    return jnp.dot(stacked, other[...], preferred_element_type=f32)
+def both_sides(table, other, cells, half):
+    left = jnp.dot(table[...], cells[...], preferred_element_type=f32).astype(bf16)
+    for b in range(B):
+        half[F * b : F * b + F, :F] = left[:F, F * b : F * b + F]
+        half[F * b : F * b + F, F:] = left[F:, F * b : F * b + F]
+    return jnp.dot(half[...], other[...], preferred_element_type=f32)
 
 
 def slots_kernel(corner, load, amp, ext, probe, fwd, inv, grad, psum,
-                 patch0, patch1, cov, exit_s, miss0, miss1, chi_s):
+                 patch0, patch1, cov, exit_s, half0, half1, miss0, miss1, chi_s):
     lane=lax.broadcasted_iota(jnp.int32,(CH,128),1)
     n=load[0]
     top=lax.axis_index("row")*F-F//2; left=lax.axis_index("col")*F-F//2
@@ -55,7 +54,7 @@
                 pr=probe[0,rows,:]; pi=probe[1,rows,:]
                 exit_s[rows,F*b:F*b+F]=(pr*re-pi*im).astype(bf16)
                 exit_s[pl.ds(F+i*CH,CH),F*b:F*b+F]=(pr*im+pi*re).astype(bf16)
-        far=both_sides(fwd,inv,exit_s)
+        far=both_sides(fwd,inv,exit_s,half0)
         for b in range(B):
             kk=jnp.minimum(B*g+b,15)
             fr=far[F*b:F*b+F,:F]; fi=far[F*b:F*b+F,F:]
@@ -63,7 +62,7 @@
             miss[:F,F*b:F*b+F]=(fr*ratio).astype(bf16)
             miss[F:,F*b:F*b+F]=(fi*ratio).astype(bf16)
     def back_(g,patch,miss):
-        chi=both_sides(inv,fwd,miss)
+        chi=both_sides(inv,fwd,miss,half1)
         chi_s[...]=chi
         for i in range(F//CH):
             rows=pl.ds(i*CH,CH)
@@ -101,13 +100,17 @@
         back_(2*j+1,patch1,miss1)
         front(2*j+2,patch0,miss0)
         return 0
-    lax.fori_loop(0,pairs,it,0)
+    lax.fori_loop(0,pairs-1,it,0)
+    back_(2*pairs-2,patch0,miss0)
+    front(2*pairs-1,patch1,miss1)
+    back_(2*pairs-1,patch1,miss1)
 def slots(corner,load,amp,ext,probe,fwd,inv):
     V=pl.BlockSpec(memory_space=pltpu.VMEM); S=pl.BlockSpec(memory_space=pltpu.SMEM)
     return pl.pallas_call(slots_kernel,
         out_shape=(jax.ShapeDtypeStruct((3,4,ROWS,128),f32),jax.ShapeDtypeStruct((3,F,F),f32)),
         in_specs=[S,S,V,V,V,V,V], out_specs=(V,V),
         scratch_shapes=[pltpu.VMEM((B,2,F,F),f32),pltpu.VMEM((B,2,F,F),f32),pltpu.VMEM((F,F),f32),pltpu.VMEM((2*F,B*F),bf16),
+            pltpu.VMEM((B*F,2*F),bf16),pltpu.VMEM((B*F,2*F),bf16),
             pltpu.VMEM((2*F,B*F),bf16),pltpu.VMEM((2*F,B*F),bf16),pltpu.VMEM((B*F,2*F),f32)],
         compiler_params=pltpu.CompilerParams(vmem_limit_bytes=24*2**20),
     )(corner,load,amp,ext,probe,fwd,inv)

time: 136 us -> 133 us (0.978)
  Pallas kernels: 131 us -> 128 us
    pallas_call x2, Pallas kernels: 99.5 us -> 76.5 us  [step(): pl.pallas_call(functools.partial(step_kernel, last), out_shape=(jax.Shape...]
    pallas_call x2, Pallas kernels: 11.3 us -> 31.2 us  [slots(): pl.pallas_call(slots_kernel, out_shape=(jax.ShapeDtypeStruct((3, 4, ROWS,...]
where the time goes in v9:
time: 133 us
  Pallas kernels  128 us (96%)
  local copies, waits for them, and re-layouts  2.93 us (2%)
  between operations  1.55 us (1%)
    pallas_call x2, Pallas kernels, step(): pl.pallas_call(functools.partial(step_kernel, last), out_shape=(jax.Shape...  76.5 us
    pallas_call x2, Pallas kernels, slots(): pl.pallas_call(slots_kernel, out_shape=(jax.ShapeDtypeStruct((3, 4, ROWS,...  31.2 us
    pallas_call x1, Pallas kernels, open_halo(): pl.pallas_call(open_kernel, out_shape=jax.ShapeDtypeStruct((2, 4, ROWS, 1...  20.6 us
    unnamed x14, local copies, waits for them, and re-layouts  2.93 us

profile of v9, /device:TPU:1, one launch (start us, length us, event | category | flops | bytes accessed | tf_op | source)
XLA Modules:
  0.0 132.8 jit_solution(17769727330936043315)
XLA Ops:
  0.6 0.0 copy-start.2
  0.6 0.0 copy-start.3
  0.7 0.0 copy-start.1
  0.7 0.0 copy-start
  1.5 0.0 copy-start.4
  1.5 1.3 copy-done.4
  2.8 0.0 copy-start.5
  2.8 20.6 %shard_map.86.ext.old = f32[2,4,768,128]{3,2,1,0:T(8,128)S(1)} custom-call(f32[2,256,256]{2,1,0:T(8,128)S(1)} %copy-done.4), custom_call_target="tpu_custom_call" | custom-call | tf_op jit(solution)/shard_map/pallas_call | solution.py:440
  23.4 0.0 copy-done.2
  23.4 0.0 copy-done.3
  23.5 0.0 copy-done.1
  23.5 0.0 copy-done
  23.5 0.0 copy-done.5
  23.5 15.5 %shard_map.87 = (f32[3,4,768,128]{3,2,1,0:T(8,128)S(1)}, f32[3,256,256]{2,1,0:T(8,128)S(1)}) custom-call(s32[2,16]{1,0:T(2,128)S(1)} %bitcast.9, s32[1]{0:T(128)} %bitcast.5.load, bf16[16,256,256]{2,1,0:T(8,128)(2,1)S(1)} %bitcast.7, f32[2,4,768,128]{3,2,1,0:T(8,128)S(1)} %shard_map.86.ext.old, f32[2,256,256]{2,1,0:T(8,128)S(1)} %copy-done.1, ...), custom_call_target="tpu_custom_call" | custom-call | tf_op jit(solution)/shard_map/pallas_call | solution.py:109
  39.0 39.0 %shard_map.88 = (f32[2,4,768,128]{3,2,1,0:T(8,128)S(1)}, f32[2,256,256]{2,1,0:T(8,128)S(1)}) custom-call(f32[3,4,768,128]{3,2,1,0:T(8,128)S(1)} %get-tuple-element.8.grad, f32[3,256,256]{2,1,0:T(8,128)S(1)} %get-tuple-element.9.psum, f32[2,4,768,128]{3,2,1,0:T(8,128)S(1)} %shard_map.86.ext.old, f32[2,256,256]{2,1,0:T(8,128)S(1)} %copy-done.1), custom_call_target="tpu_custom_call" | custom-call | tf_op jit(solution)/shard_map/pallas_call | solution.py:459
  78.1 15.7 %shard_map.89 = (f32[3,4,768,128]{3,2,1,0:T(8,128)S(1)}, f32[3,256,256]{2,1,0:T(8,128)S(1)}) custom-call(s32[2,16]{1,0:T(2,128)S(1)} %bitcast.10, s32[1]{0:T(128)} %bitcast.6.load, bf16[16,256,256]{2,1,0:T(8,128)(2,1)S(1)} %bitcast.8, f32[2,4,768,128]{3,2,1,0:T(8,128)S(1)} %get-tuple-element.10.ext.old, f32[2,256,256]{2,1,0:T(8,128)S(1)} %get-tuple-element.11.probe, ...), custom_call_target="tpu_custom_call" | custom-call | tf_op jit(solution)/shard_map/pallas_call | solution.py:109
  93.8 37.4 %shard_map.90 = (f32[2,256,256]{2,1,0:T(8,128)S(1)}, f32[2,256,256]{2,1,0:T(8,128)S(1)}) custom-call(f32[3,4,768,128]{3,2,1,0:T(8,128)S(1)} %get-tuple-element.12.grad, f32[3,256,256]{2,1,0:T(8,128)S(1)} %get-tuple-element.13.psum, f32[2,4,768,128]{3,2,1,0:T(8,128)S(1)} %get-tuple-element.10.ext.old, f32[2,256,256]{2,1,0:T(8,128)S(1)} %get-tuple-element.11.probe), custom_call_target="tpu_custom_call" | custom-call | tf_op jit(solution)/shard_map/pallas_call | solution.py:459
  131.2 0.8 copy.12
  132.0 0.8 copy.13
Async XLA Ops:
  0.6 22.8 %copy-start.2 = (bf16[512,512]{1,0:T(8,128)(2,1)S(1)}, bf16[512,512]{1,0:T(8,128)(2,1)}, u32[]{:S(2)}) copy-start(bf16[512,512]{1,0:T(8,128)(2,1)} %constant.5.clone.inv) | copy-start | bytes 1572868
  0.6 22.8 %copy-start.3 = (bf16[512,512]{1,0:T(8,128)(2,1)S(1)}, bf16[512,512]{1,0:T(8,128)(2,1)}, u32[]{:S(2)}) copy-start(bf16[512,512]{1,0:T(8,128)(2,1)} %constant.4.clone.fwd) | copy-start | bytes 1572868
  0.7 22.8 %copy-start.1 = (f32[2,256,256]{2,1,0:T(8,128)S(1)}, f32[2,256,256]{2,1,0:T(8,128)}, u32[]{:S(2)}) copy-start(f32[2,256,256]{2,1,0:T(8,128)} %probe.3) | copy-start | bytes 1572868
  0.7 22.8 %copy-start = (bf16[1,1,16,256,256]{4,3,2,1,0:T(8,128)(2,1)S(1)}, bf16[1,1,16,256,256]{4,3,2,1,0:T(8,128)(2,1)}, u32[]{:S(2)}) copy-start(bf16[1,1,16,256,256]{4,3,2,1,0:T(8,128)(2,1)} %param.9) | copy-start | bytes 6291460
  1.5 1.3 copy-start.4
  2.8 20.7 %copy-start.5 = (s32[1,1,16,2]{2,3,1,0:T(2,128)S(1)}, s32[1,1,16,2]{2,3,1,0:T(2,128)}, u32[]{:S(2)}) copy-start(s32[1,1,16,2]{2,3,1,0:T(2,128)} %param.7) | copy-start | bytes 388

commit v10 on v9

--- a/solution.py
+++ b/solution.py
@@ -151,6 +151,7 @@
         self.near_rim, self.far_rim = 3 - 3 * self.core, 3 * self.core
         self.near_edge, self.far_edge = 2 - self.core, 1 + self.core
         self.along_x = [(row, (self.x + d) % 4 * 4 + col % 4) for d in (1, 2, 3)]
+        self.across = [(row, (self.x + d) % 4 * 4 + col % 4 + 1 - 2 * self.core) for d in (1, 2, 3)]
         self.along_y = [(z_lo * 4 + (self.y + d) % 4, col) for d in (1, 2, 3)]
         self.along_z = []
         for d in (1, 2, 3):
@@ -298,9 +299,9 @@
 
 def step_kernel(last, grad, psum, old, probe, new, probe_new, *scratch):
     from_up, from_down, sides_in, far_in, side, strips, relay, halo_relay = scratch[:8]
-    acc0, buf0, acc1, buf1, acc2, buf2, buf3, send_sem, recv_sem = scratch[8:]
+    acc1, buf1, acc2, buf2, buf3, send_sem, recv_sem = scratch[8:]
     at = Places()
-    meet((*at.around, *at.along_x, *at.along_y, *at.along_z))
+    meet((*at.around, *at.along_x, *at.across, *at.along_y, *at.along_z))
     send = Sender(send_sem, recv_sem)
     above, below = at.above, at.below
     up, down = (above, below), (below, above)
@@ -311,7 +312,14 @@
     far_edge = pl.ds(at.far_edge, 1)
     near_part, far_part = pl.ds(at.near_edge - 1, 1), pl.ds(at.far_edge - 1, 1)
 
-    s0 = send(psum.at[:, pl.ds(128 - base, 128), :], buf0, at.twin)
+    s1 = []
+    for k, (peer, core, d) in enumerate(
+        [(at.along_x[d - 1], at.core, d) for d in (1, 2, 3)]
+        + [(at.across[d - 1], 1 - at.core, d) for d in (1, 2, 3)]
+        + [(at.twin, 1 - at.core, 0)]
+    ):
+        rows = pl.ds(core * 128 + (at.x + d) % 4 * 32, 32)
+        s1.append(send(psum.at[:, rows, :], buf1.at[k], peer))
     twins = send(grad.at[:, near_rim, : 2 * F, :], sides_in.at[at.core], at.twin)
     corners = [
         [
@@ -325,12 +333,6 @@
         send(grad.at[:, far_edge, ABOVE, :], from_down.at[:, far_part], at.up, *up),
         send(grad.at[:, far_edge, BELOW, :], from_up.at[:, far_part], at.down, *down),
     ]
-    arrive([s0])
-    acc0[...] = psum[:, pl.ds(base, 128), :] + buf0[...]
-    s1 = [
-        send(acc0.at[:, pl.ds((at.x + d) % 4 * 32, 32), :], buf1.at[d - 1], at.along_x[d - 1])
-        for d in (1, 2, 3)
-    ]
     arrive([twins])
     for ch in range(3):
         for k, rows in enumerate((ABOVE, BELOW)):
@@ -357,7 +359,10 @@
         there = sides_in.at[1 - at.core, pl.ds(ch, 1), :, INNER, :]
         rims.append(send(side.at[pl.ds(ch, 1)], there, at.far, at.aside, at.aside))
     arrive(s1)
-    acc1[...] = acc0[:, pl.ds(at.x * 32, 32), :] + buf1[0] + buf1[1] + buf1[2]
+    total = psum[:, pl.ds(base_x, 32), :]
+    for k in range(7):
+        total = total + buf1[k]
+    acc1[...] = total
     s2 = [
         send(acc1.at[:, pl.ds((at.y + d) % 4 * 8, 8), :], buf2.at[d - 1], at.along_y[d - 1])
         for d in (1, 2, 3)
@@ -414,16 +419,13 @@
         arriving, halo = (relays, passing, strips_out), halo + rest
     arrive(s4)
     part = probe_new.at[:, pl.ds(base_x, 32), :]
-    s5 = [send(part, part, peer) for peer in at.along_x]
+    s5 = [send(part, part, peer) for peer in (*at.along_x, *at.across, at.twin)]
     if not last:
         halo += pass_on_halo(send, at, new, halo_relay, arriving)
-    arrive(s5)
-    part = probe_new.at[:, pl.ds(base, 128), :]
-    s6 = send(part, part, at.twin)
     if last:
         finish_far()
         finish_near()
-    arrive([s6])
+    arrive(s5)
     if not last:
         arrive(halo)
     send.close()
@@ -455,7 +457,7 @@
 
 def step(last, grad, psum, old, probe):
     shape = (2, F, F) if last else (2, 4, ROWS, 128)
-    copies = 35 if last else 57
+    copies = 41 if last else 63
     return pl.pallas_call(
         functools.partial(step_kernel, last),
         out_shape=(jax.ShapeDtypeStruct(shape, f32), jax.ShapeDtypeStruct((2, F, F), f32)),
@@ -470,10 +472,8 @@
             pltpu.VMEM((2, 3, 1, HALF, 128), f32),
             pltpu.VMEM((3, 1, HALF, 128), f32),
             pltpu.VMEM((1, 1, HALF, 128), f32),
-            pltpu.VMEM((3, 128, F), f32),
-            pltpu.VMEM((3, 128, F), f32),
             pltpu.VMEM((3, 32, F), f32),
-            pltpu.VMEM((3, 3, 32, F), f32),
+            pltpu.VMEM((7, 3, 32, F), f32),
             pltpu.VMEM((3, 8, F), f32),
             pltpu.VMEM((3, 3, 8, F), f32),
             pltpu.VMEM((4, 3, 8, F), f32),

time: 133 us -> 135 us (1.015)
  Pallas kernels: 128 us -> 130 us
where the time goes in v10:
time: 135 us; the launch traced here: 134 us
  Pallas kernels  130 us (96%)
  local copies, waits for them, and re-layouts  2.93 us (2%)
  between operations  1.55 us (1%)
    pallas_call x2, Pallas kernels, step(): pl.pallas_call(functools.partial(step_kernel, last), out_shape=(jax.Shape...  77.7 us
    pallas_call x2, Pallas kernels, slots(): pl.pallas_call(slots_kernel, out_shape=(jax.ShapeDtypeStruct((3, 4, ROWS,...  31.3 us
    pallas_call x1, Pallas kernels, open_halo(): pl.pallas_call(open_kernel, out_shape=jax.ShapeDtypeStruct((2, 4, ROWS, 1...  20.6 us
    unnamed x14, local copies, waits for them, and re-layouts  2.93 us

profile of v10, /device:TPU:1, one launch (start us, length us, event | category | flops | bytes accessed | tf_op | source)
XLA Modules:
  0.0 134.1 jit_solution(14045548968462659595)
XLA Ops:
  0.6 0.0 copy-start.2
  0.6 0.0 copy-start.3
  0.7 0.0 copy-start.1
  0.7 0.0 copy-start
  1.5 0.0 copy-start.4
  1.5 1.3 copy-done.4
  2.8 0.0 copy-start.5
  2.8 20.6 %shard_map.86.ext.old = f32[2,4,768,128]{3,2,1,0:T(8,128)S(1)} custom-call(f32[2,256,256]{2,1,0:T(8,128)S(1)} %copy-done.4), custom_call_target="tpu_custom_call" | custom-call | tf_op jit(solution)/shard_map/pallas_call | solution.py:442
  23.4 0.0 copy-done.2
  23.4 0.0 copy-done.3
  23.5 0.0 copy-done.1
  23.5 0.0 copy-done
  23.5 0.0 copy-done.5
  23.5 15.6 %shard_map.87 = (f32[3,4,768,128]{3,2,1,0:T(8,128)S(1)}, f32[3,256,256]{2,1,0:T(8,128)S(1)}) custom-call(s32[2,16]{1,0:T(2,128)S(1)} %bitcast.9, s32[1]{0:T(128)} %bitcast.5.load, bf16[16,256,256]{2,1,0:T(8,128)(2,1)S(1)} %bitcast.7, f32[2,4,768,128]{3,2,1,0:T(8,128)S(1)} %shard_map.86.ext.old, f32[2,256,256]{2,1,0:T(8,128)S(1)} %copy-done.1, ...), custom_call_target="tpu_custom_call" | custom-call | tf_op jit(solution)/shard_map/pallas_call | solution.py:109
  39.0 39.6 %shard_map.88 = (f32[2,4,768,128]{3,2,1,0:T(8,128)S(1)}, f32[2,256,256]{2,1,0:T(8,128)S(1)}) custom-call(f32[3,4,768,128]{3,2,1,0:T(8,128)S(1)} %get-tuple-element.8.grad, f32[3,256,256]{2,1,0:T(8,128)S(1)} %get-tuple-element.9.psum, f32[2,4,768,128]{3,2,1,0:T(8,128)S(1)} %shard_map.86.ext.old, f32[2,256,256]{2,1,0:T(8,128)S(1)} %copy-done.1), custom_call_target="tpu_custom_call" | custom-call | tf_op jit(solution)/shard_map/pallas_call | solution.py:461
  78.6 15.7 %shard_map.89 = (f32[3,4,768,128]{3,2,1,0:T(8,128)S(1)}, f32[3,256,256]{2,1,0:T(8,128)S(1)}) custom-call(s32[2,16]{1,0:T(2,128)S(1)} %bitcast.10, s32[1]{0:T(128)} %bitcast.6.load, bf16[16,256,256]{2,1,0:T(8,128)(2,1)S(1)} %bitcast.8, f32[2,4,768,128]{3,2,1,0:T(8,128)S(1)} %get-tuple-element.10.ext.old, f32[2,256,256]{2,1,0:T(8,128)S(1)} %get-tuple-element.11.probe, ...), custom_call_target="tpu_custom_call" | custom-call | tf_op jit(solution)/shard_map/pallas_call | solution.py:109
  94.3 38.1 %shard_map.90 = (f32[2,256,256]{2,1,0:T(8,128)S(1)}, f32[2,256,256]{2,1,0:T(8,128)S(1)}) custom-call(f32[3,4,768,128]{3,2,1,0:T(8,128)S(1)} %get-tuple-element.12.grad, f32[3,256,256]{2,1,0:T(8,128)S(1)} %get-tuple-element.13.psum, f32[2,4,768,128]{3,2,1,0:T(8,128)S(1)} %get-tuple-element.10.ext.old, f32[2,256,256]{2,1,0:T(8,128)S(1)} %get-tuple-element.11.probe), custom_call_target="tpu_custom_call" | custom-call | tf_op jit(solution)/shard_map/pallas_call | solution.py:461
  132.5 0.8 copy.12
  133.3 0.8 copy.13
Async XLA Ops:
  0.6 22.8 %copy-start.2 = (bf16[512,512]{1,0:T(8,128)(2,1)S(1)}, bf16[512,512]{1,0:T(8,128)(2,1)}, u32[]{:S(2)}) copy-start(bf16[512,512]{1,0:T(8,128)(2,1)} %constant.5.clone.inv) | copy-start | bytes 1572868
  0.6 22.8 %copy-start.3 = (bf16[512,512]{1,0:T(8,128)(2,1)S(1)}, bf16[512,512]{1,0:T(8,128)(2,1)}, u32[]{:S(2)}) copy-start(bf16[512,512]{1,0:T(8,128)(2,1)} %constant.4.clone.fwd) | copy-start | bytes 1572868
  0.7 22.8 %copy-start.1 = (f32[2,256,256]{2,1,0:T(8,128)S(1)}, f32[2,256,256]{2,1,0:T(8,128)}, u32[]{:S(2)}) copy-start(f32[2,256,256]{2,1,0:T(8,128)} %probe.3) | copy-start | bytes 1572868
  0.7 22.8 %copy-start = (bf16[1,1,16,256,256]{4,3,2,1,0:T(8,128)(2,1)S(1)}, bf16[1,1,16,256,256]{4,3,2,1,0:T(8,128)(2,1)}, u32[]{:S(2)}) copy-start(bf16[1,1,16,256,256]{4,3,2,1,0:T(8,128)(2,1)} %param.9) | copy-start | bytes 6291460
  1.5 1.3 copy-start.4
  2.8 20.7 %copy-start.5 = (s32[1,1,16,2]{2,3,1,0:T(2,128)S(1)}, s32[1,1,16,2]{2,3,1,0:T(2,128)}, u32[]{:S(2)}) copy-start(s32[1,1,16,2]{2,3,1,0:T(2,128)} %param.7) | copy-start | bytes 388
